TPU v7x, 128 devices: a whole 4x4x4 slice. The times are simulated.
128 devices in a mesh: layer: 4 (over x), tile: 32 (over z, y, core).
Axes of the slice: x: 4, y: 4, z: 4, core: 2. Of those that a mesh axis runs over, the one named last changes fastest.
Arguments:
- frames: bfloat16 [6, 32, 16, 8, 256], P(None, 'tile'), may hold values from -6 to 6
- weight: bfloat16 [4, 4608, 1024], P('layer'), may hold values from -0.09375 to 0.09375
- cotangent: bfloat16 [6, 32, 16, 8, 256], P(None, 'tile'), may hold values from -6 to 6
Outputs:
- hidden_maps: bfloat16 [4, 6, 32, 16, 8, 256], P('layer', None, 'tile')
- grad_inputs: bfloat16 [4, 6, 32, 16, 8, 256], P('layer', None, 'tile')
- weight_grad: float32 [4, 4608, 1024], P('layer', 'tile')
All inputs are finite; a program needn't handle non-finite values.
Results may differ from a plain program's by a relative error of at most 0.02.
Values may be sent and summed in bfloat16 or wider, within the bound.
A program may use at most 128 MiB of HBM per device.

v0:
```python
import jax
import jax.numpy as jnp
from jax import lax
from jax.sharding import PartitionSpec as P

TX = 8


FORGET_SHIFT = 1.0


def shifted(value, axis, steps):
    count = lax.axis_size(axis)
    first, last = (max(0, -steps), min(count, count - steps))
    return lax.ppermute(value, axis, [(source, source + steps) for source in range(first, last)])


def cell_forward(gate_sums, cell_prev):
    channels = cell_prev.shape[-1]
    in_gate = jax.nn.sigmoid(gate_sums[:, :channels])
    forget = jax.nn.sigmoid(gate_sums[:, channels : 2 * channels] + FORGET_SHIFT)
    out_gate = jax.nn.sigmoid(gate_sums[:, 2 * channels : 3 * channels])
    update = jnp.tanh(gate_sums[:, 3 * channels :])
    cell_state = forget * cell_prev + in_gate * update
    hidden = out_gate * jnp.tanh(cell_state)
    return (jnp.concatenate([in_gate, forget, out_gate, update], axis=1), cell_state, hidden)


def cell_backward(activations, cell_state, cell_prev, grad_hidden, carried):
    channels = cell_state.shape[-1]
    in_gate = activations[:, :channels]
    forget = activations[:, channels : 2 * channels]
    out_gate = activations[:, 2 * channels : 3 * channels]
    update = activations[:, 3 * channels :]
    squashed = jnp.tanh(cell_state)
    grad_cell = grad_hidden * out_gate * (1.0 - squashed * squashed) + carried
    grad_gates = jnp.concatenate(
        [
            grad_cell * update * in_gate * (1.0 - in_gate),
            grad_cell * cell_prev * forget * (1.0 - forget),
            grad_hidden * squashed * out_gate * (1.0 - out_gate),
            grad_cell * in_gate * (1.0 - update * update),
        ],
        axis=1,
    )
    return (grad_gates, grad_cell * forget)


def patch_rows(padded, tile_rows, tile_cols):
    pieces = [
        padded[tap_row : tap_row + tile_rows, tap_col : tap_col + tile_cols]
        for tap_row in range(3)
        for tap_col in range(3)
    ]
    return jnp.concatenate(pieces, axis=-1).reshape(tile_rows * tile_cols, -1)


def flipped_rows(padded, tile_rows, tile_cols):
    pieces = [
        padded[2 - tap_row : 2 - tap_row + tile_rows, 2 - tap_col : 2 - tap_col + tile_cols]
        for tap_row in range(3)
        for tap_col in range(3)
    ]
    return jnp.concatenate(pieces, axis=-1).reshape(tile_rows * tile_cols, -1)


def store_at(store, value, slot_index, is_live):
    previous = lax.dynamic_index_in_dim(store, slot_index, 0, keepdims=False)
    return lax.dynamic_update_index_in_dim(
        store, jnp.where(is_live, value, previous), slot_index, 0
    )


def extend(tile_map):
    column = lax.axis_index("tile") % TX
    rim_table = (
        (TX + 1, tile_map[-1:, -1:], 0),
        (TX, tile_map[-1:], -1),
        (TX - 1, tile_map[-1:, :1], TX - 1),
        (1, tile_map[:, -1:], 0),
        (-1, tile_map[:, :1], TX - 1),
        (1 - TX, tile_map[:1, -1:], 0),
        (-TX, tile_map[:1], -1),
        (-TX - 1, tile_map[:1, :1], TX - 1),
    )
    pieces = []
    for offset, rim_slice, border in rim_table:
        arrived = shifted(rim_slice, "tile", offset)
        if border >= 0:
            arrived = jnp.where(column == border, jnp.zeros_like(arrived), arrived)
        pieces.append(arrived)
    top_row = jnp.concatenate(pieces[0:3], axis=1)
    middle_rows = jnp.concatenate([pieces[3], tile_map, pieces[4]], axis=1)
    bottom_row = jnp.concatenate(pieces[5:8], axis=1)
    return jnp.concatenate([top_row, middle_rows, bottom_row], axis=0)


def local(frames, weight, cotangent):
    step_count, _, tile_rows, tile_cols, channels = frames.shape
    layer_count = lax.axis_size("layer")
    layer_index = lax.axis_index("layer")
    kernel = weight[0]
    gate_count = kernel.shape[1]
    pixels = tile_rows * tile_cols
    frame_maps = frames[:, 0]
    top_grads = cotangent[:, 0]
    wave_count = step_count + layer_count - 1

    def forward_step(state, wave_step):
        hidden, cell_state, from_below, hid_store, cell_store, act_store, pad_store = state
        time_step = wave_step - layer_index
        is_live = (time_step >= 0) & (time_step < step_count)
        slot_index = jnp.clip(time_step, 0, step_count - 1)
        own_frame = lax.dynamic_index_in_dim(frame_maps, slot_index, 0, keepdims=False)
        layer_input = jnp.where(layer_index == 0, own_frame, from_below)
        stacked = jnp.concatenate([layer_input, hidden], axis=-1)
        padded = extend(stacked)
        gate_sums = jnp.dot(
            patch_rows(padded, tile_rows, tile_cols), kernel, preferred_element_type=jnp.float32
        )
        activations, fresh_cell, fresh = cell_forward(gate_sums, cell_state)
        fresh = fresh.astype(jnp.bfloat16).reshape(tile_rows, tile_cols, channels)
        hidden = jnp.where(is_live, fresh, hidden)
        cell_state = jnp.where(is_live, fresh_cell, cell_state)
        hid_store = store_at(hid_store, hidden, slot_index, is_live)
        cell_store = store_at(cell_store, cell_state, slot_index + 1, is_live)
        act_store = store_at(act_store, activations, slot_index, is_live)
        pad_store = store_at(pad_store, padded, slot_index, is_live)
        from_below = shifted(hidden, "layer", 1)
        return ((hidden, cell_state, from_below, hid_store, cell_store, act_store, pad_store), None)

    start_state = (
        jnp.zeros((tile_rows, tile_cols, channels), jnp.bfloat16),
        jnp.zeros((pixels, channels), jnp.float32),
        jnp.zeros((tile_rows, tile_cols, channels), jnp.bfloat16),
        jnp.zeros((step_count, tile_rows, tile_cols, channels), jnp.bfloat16),
        jnp.zeros((step_count + 1, pixels, channels), jnp.float32),
        jnp.zeros((step_count, pixels, gate_count), jnp.float32),
        jnp.zeros((step_count, tile_rows + 2, tile_cols + 2, 2 * channels), jnp.bfloat16),
    )
    final_state, _ = lax.scan(forward_step, start_state, jnp.arange(wave_count, dtype=jnp.int32))
    hid_store, cell_store, act_store, pad_store = (
        final_state[3],
        final_state[4],
        final_state[5],
        final_state[6],
    )
    flipped = (
        kernel.reshape(9, 2 * channels, gate_count)
        .transpose(0, 2, 1)
        .reshape(9 * gate_count, 2 * channels)
    )

    def backward_step(state, wave_step):
        from_above, recurrent, carried, grad_store, gate_store = state
        time_step = step_count - 1 - wave_step + (layer_count - 1 - layer_index)
        is_live = (time_step >= 0) & (time_step < step_count)
        slot_index = jnp.clip(time_step, 0, step_count - 1)
        from_top = lax.dynamic_index_in_dim(top_grads, slot_index, 0, keepdims=False)
        upstream = jnp.where(layer_index == layer_count - 1, from_top, from_above)
        grad_hidden = upstream.astype(jnp.float32).reshape(pixels, channels) + recurrent
        activations = lax.dynamic_index_in_dim(act_store, slot_index, 0, keepdims=False)
        cell_state = lax.dynamic_index_in_dim(cell_store, slot_index + 1, 0, keepdims=False)
        cell_prev = lax.dynamic_index_in_dim(cell_store, slot_index, 0, keepdims=False)
        grad_gates, next_carried = cell_backward(
            activations, cell_state, cell_prev, grad_hidden, carried
        )
        grad_gates = grad_gates.astype(jnp.bfloat16)
        padded = extend(grad_gates.reshape(tile_rows, tile_cols, gate_count))
        grad_stacked = jnp.dot(
            flipped_rows(padded, tile_rows, tile_cols), flipped, preferred_element_type=jnp.float32
        )
        grad_input = (
            grad_stacked[:, :channels].astype(jnp.bfloat16).reshape(tile_rows, tile_cols, channels)
        )
        recurrent = jnp.where(is_live, grad_stacked[:, channels:], recurrent)
        carried = jnp.where(is_live, next_carried, carried)
        grad_store = store_at(grad_store, grad_input, slot_index, is_live)
        gate_store = store_at(gate_store, grad_gates, slot_index, is_live)
        from_above = shifted(grad_input, "layer", -1)
        return ((from_above, recurrent, carried, grad_store, gate_store), None)

    back_state = (
        jnp.zeros((tile_rows, tile_cols, channels), jnp.bfloat16),
        jnp.zeros((pixels, channels), jnp.float32),
        jnp.zeros((pixels, channels), jnp.float32),
        jnp.zeros((step_count, tile_rows, tile_cols, channels), jnp.bfloat16),
        jnp.zeros((step_count, pixels, gate_count), jnp.bfloat16),
    )
    back_final, _ = lax.scan(backward_step, back_state, jnp.arange(wave_count, dtype=jnp.int32))
    grad_store, gate_store = (back_final[3], back_final[4])
    all_patches = jax.vmap(lambda padded: patch_rows(padded, tile_rows, tile_cols))(
        pad_store
    ).reshape(step_count * pixels, -1)
    all_gates = gate_store.reshape(step_count * pixels, gate_count)
    weight_grad = lax.psum_scatter(
        lax.dot_general(
            all_patches, all_gates, (((0,), (0,)), ((), ())), preferred_element_type=jnp.float32
        ).astype(jnp.bfloat16),
        "tile",
        scatter_dimension=0,
        tiled=True,
    ).astype(jnp.float32)
    return (hid_store[None, :, None], grad_store[None, :, None], weight_grad[None])


def solution(mesh):
    in_specs = (
        P(None, "tile", None, None, None),
        P("layer", None, None),
        P(None, "tile", None, None, None),
    )
    out_specs = (
        P("layer", None, "tile", None, None, None),
        P("layer", None, "tile", None, None, None),
        P("layer", "tile", None),
    )
    return jax.shard_map(local, mesh=mesh, in_specs=in_specs, out_specs=out_specs, check_vma=False)
```

profile of v0, /device:TPU:1, one launch (start us, length us, event | category | flops | bytes accessed | tf_op | source)
XLA Modules:
  0.0 1004.6 jit_solution(16972893955607075419)
XLA Ops:
  7.3 12.7 %copy.6 = bf16[9,512,1024]{1,2,0:T(8,128)(2,1)} copy(bf16[9,512,1024]{2,1,0:T(8,128)(2,1)} %bitcast.215) | data formatting | bytes 18874368 | tf_op jit(solution)/shard_map/reshape;squeeze | solution.py:149
  23.6 426.3 %while.48 = (s32[]{:T(128)}, bf16[16,8,256]{2,1,0:T(8,128)(2,1)S(1)}, f32[128,256]{1,0:T(8,128)S(1)}, bf16[16,8,256]{2,1,0:T(8,128)(2,1)S(1)}, bf16[6,16,8,256]{...) while((s32[]{:T(128)}, ...), condition=%wide.region_1.2_spmd.clone, body=%wide.region_0.1_spmd.clone.sunk | while | flops 1214242816 | bytes 21263188 | solution.py:141
  82.5 7.0 collective-permute-start.5
  129.4 7.8 collective-permute-start.5
  177.2 7.8 collective-permute-start.5
  224.9 7.8 collective-permute-start.5
  239.2 5.9 collective-permute-start.7
  272.7 7.8 collective-permute-start.5
  320.4 7.8 collective-permute-start.5
  368.2 7.8 collective-permute-start.5
  415.9 7.8 collective-permute-start.5
  430.2 5.9 collective-permute-start.7
  455.4 429.5 %while.49 = (s32[]{:T(128)}, bf16[16,8,256]{2,1,0:T(8,128)(2,1)S(1)}, f32[128,256]{1,0:T(8,128)S(1)}, f32[128,256]{1,0:T(8,128)S(1)}, bf16[6,16,8,256]{3,2,1,0:T...) while((s32[]{:T(128)}, ...), condition=%wide.region_3.4_spmd.clone, body=%wide.region_2.3_spmd.clone.sunk | while | flops 1220423680 | bytes 24552292 | solution.py:190
  464.6 7.2 collective-permute-start.11
  507.6 8.0 collective-permute-start.9
  556.9 6.0 collective-permute-start.9
  604.2 6.5 collective-permute-start.9
  651.7 6.3 collective-permute-start.9
  698.9 6.5 collective-permute-start.9
  746.4 6.3 collective-permute-start.9
  793.7 6.5 collective-permute-start.9
  841.2 6.3 collective-permute-start.9
  885.0 13.1 %convolution_convert_fusion = bf16[4608,1024]{1,0:T(8,128)(2,1)} fusion(bf16[768,4608]{1,0:T(8,128)(2,1)} %bitcast.247, bf16[768,1024]{1,0:T(8,128)(2,1)S(1)} %bitcast.242), kind=kOutput, calls=%fused_computation.150 | convolution fusion | flops 7252475904 | bytes 18087936 | tf_op jit(solution)/shard_map/dot_general | solution.py:197
  898.1 97.8 %reduce-scatter.2.cloned.1.call-done = bf16[144,1024]{1,0:T(8,128)(2,1)} async-done(((bf16[4608,1024]{1,0:T(8,128)(2,1)}), bf16[144,1024]{1,0:T(8,128)(2,1)}) %reduce-scatter.2.cloned.1.call-update) | async-done | bytes 294928 | tf_op jit(solution)/shard_map/reduce_scatter | solution.py:196
  (918 shorter events, 715.5 us)
Async XLA Ops:
  7.2 988.8 %reduce-scatter.2.cloned.1.call-start = ((), (), s32[]{:S(2)}) async-start(), calls=%async_computation.1 | async-start | bytes 9732096 | tf_op jit(solution)/shard_map/reduce_scatter | solution.py:196
  27.7 28.7 %collective-permute-start.1 = (bf16[1,8,512]{2,1,0:T(8,128)(2,1)S(1)}, bf16[1,8,512]{2,1,0:T(8,128)(2,1)S(1)}, u32[]{:S(2)}, u32[]{:S(2)}) collective-permute-start(bf16[1,8,512]{2,1,0:T(8,128)(2,1)S(1)} %get-tuple-element.754), channel_id=1, source_target_pairs={{8,0},{9,1},{10,2},{11,3},{12,4},{13,5},{14,6},{15,7},{16,8},{17,9... | collective-permute-start | bytes 24584 | tf_op jit(solution)/shard_map/while/body/eval_jaxpr/ppermute | solution.py:15
  72.8 29.8 %collective-permute-start.1 = (bf16[1,8,512]{2,1,0:T(8,128)(2,1)S(1)}, bf16[1,8,512]{2,1,0:T(8,128)(2,1)S(1)}, u32[]{:S(2)}, u32[]{:S(2)}) collective-permute-start(bf16[1,8,512]{2,1,0:T(8,128)(2,1)S(1)} %get-tuple-element.754), channel_id=1, source_target_pairs={{8,0},{9,1},{10,2},{11,3},{12,4},{13,5},{14,6},{15,7},{16,8},{17,9... | collective-permute-start | bytes 24584 | tf_op jit(solution)/shard_map/while/body/eval_jaxpr/ppermute | solution.py:15
  119.7 30.6 %collective-permute-start.1 = (bf16[1,8,512]{2,1,0:T(8,128)(2,1)S(1)}, bf16[1,8,512]{2,1,0:T(8,128)(2,1)S(1)}, u32[]{:S(2)}, u32[]{:S(2)}) collective-permute-start(bf16[1,8,512]{2,1,0:T(8,128)(2,1)S(1)} %get-tuple-element.754), channel_id=1, source_target_pairs={{8,0},{9,1},{10,2},{11,3},{12,4},{13,5},{14,6},{15,7},{16,8},{17,9... | collective-permute-start | bytes 24584 | tf_op jit(solution)/shard_map/while/body/eval_jaxpr/ppermute | solution.py:15
  122.9 27.4 %collective-permute-start.3 = (bf16[16,1,512]{2,1,0:T(2,128)(2,1)}, bf16[16,1,512]{2,1,0:T(2,128)(2,1)S(1)}, u32[]{:S(2)}, u32[]{:S(2)}) collective-permute-start(bf16[16,1,512]{2,1,0:T(2,128)(2,1)} %get-tuple-element.756), channel_id=1, source_target_pairs={{1,0},{2,1},{3,2},{4,3},{5,4},{6,5},{7,6},{8,7},{9,8},{10,9},{11,1... | collective-permute-start | bytes 49160 | tf_op jit(solution)/shard_map/while/body/eval_jaxpr/ppermute | solution.py:15
  167.5 30.6 %collective-permute-start.1 = (bf16[1,8,512]{2,1,0:T(8,128)(2,1)S(1)}, bf16[1,8,512]{2,1,0:T(8,128)(2,1)S(1)}, u32[]{:S(2)}, u32[]{:S(2)}) collective-permute-start(bf16[1,8,512]{2,1,0:T(8,128)(2,1)S(1)} %get-tuple-element.754), channel_id=1, source_target_pairs={{8,0},{9,1},{10,2},{11,3},{12,4},{13,5},{14,6},{15,7},{16,8},{17,9... | collective-permute-start | bytes 24584 | tf_op jit(solution)/shard_map/while/body/eval_jaxpr/ppermute | solution.py:15
  215.2 30.6 %collective-permute-start.1 = (bf16[1,8,512]{2,1,0:T(8,128)(2,1)S(1)}, bf16[1,8,512]{2,1,0:T(8,128)(2,1)S(1)}, u32[]{:S(2)}, u32[]{:S(2)}) collective-permute-start(bf16[1,8,512]{2,1,0:T(8,128)(2,1)S(1)} %get-tuple-element.754), channel_id=1, source_target_pairs={{8,0},{9,1},{10,2},{11,3},{12,4},{13,5},{14,6},{15,7},{16,8},{17,9... | collective-permute-start | bytes 24584 | tf_op jit(solution)/shard_map/while/body/eval_jaxpr/ppermute | solution.py:15
  218.5 27.4 %collective-permute-start.3 = (bf16[16,1,512]{2,1,0:T(2,128)(2,1)}, bf16[16,1,512]{2,1,0:T(2,128)(2,1)S(1)}, u32[]{:S(2)}, u32[]{:S(2)}) collective-permute-start(bf16[16,1,512]{2,1,0:T(2,128)(2,1)} %get-tuple-element.756), channel_id=1, source_target_pairs={{1,0},{2,1},{3,2},{4,3},{5,4},{6,5},{7,6},{8,7},{9,8},{10,9},{11,1... | collective-permute-start | bytes 49160 | tf_op jit(solution)/shard_map/while/body/eval_jaxpr/ppermute | solution.py:15
  263.0 30.6 %collective-permute-start.1 = (bf16[1,8,512]{2,1,0:T(8,128)(2,1)S(1)}, bf16[1,8,512]{2,1,0:T(8,128)(2,1)S(1)}, u32[]{:S(2)}, u32[]{:S(2)}) collective-permute-start(bf16[1,8,512]{2,1,0:T(8,128)(2,1)S(1)} %get-tuple-element.754), channel_id=1, source_target_pairs={{8,0},{9,1},{10,2},{11,3},{12,4},{13,5},{14,6},{15,7},{16,8},{17,9... | collective-permute-start | bytes 24584 | tf_op jit(solution)/shard_map/while/body/eval_jaxpr/ppermute | solution.py:15
  266.2 27.4 %collective-permute-start.3 = (bf16[16,1,512]{2,1,0:T(2,128)(2,1)}, bf16[16,1,512]{2,1,0:T(2,128)(2,1)S(1)}, u32[]{:S(2)}, u32[]{:S(2)}) collective-permute-start(bf16[16,1,512]{2,1,0:T(2,128)(2,1)} %get-tuple-element.756), channel_id=1, source_target_pairs={{1,0},{2,1},{3,2},{4,3},{5,4},{6,5},{7,6},{8,7},{9,8},{10,9},{11,1... | collective-permute-start | bytes 49160 | tf_op jit(solution)/shard_map/while/body/eval_jaxpr/ppermute | solution.py:15
  310.7 30.6 %collective-permute-start.1 = (bf16[1,8,512]{2,1,0:T(8,128)(2,1)S(1)}, bf16[1,8,512]{2,1,0:T(8,128)(2,1)S(1)}, u32[]{:S(2)}, u32[]{:S(2)}) collective-permute-start(bf16[1,8,512]{2,1,0:T(8,128)(2,1)S(1)} %get-tuple-element.754), channel_id=1, source_target_pairs={{8,0},{9,1},{10,2},{11,3},{12,4},{13,5},{14,6},{15,7},{16,8},{17,9... | collective-permute-start | bytes 24584 | tf_op jit(solution)/shard_map/while/body/eval_jaxpr/ppermute | solution.py:15
  358.5 30.6 %collective-permute-start.1 = (bf16[1,8,512]{2,1,0:T(8,128)(2,1)S(1)}, bf16[1,8,512]{2,1,0:T(8,128)(2,1)S(1)}, u32[]{:S(2)}, u32[]{:S(2)}) collective-permute-start(bf16[1,8,512]{2,1,0:T(8,128)(2,1)S(1)} %get-tuple-element.754), channel_id=1, source_target_pairs={{8,0},{9,1},{10,2},{11,3},{12,4},{13,5},{14,6},{15,7},{16,8},{17,9... | collective-permute-start | bytes 24584 | tf_op jit(solution)/shard_map/while/body/eval_jaxpr/ppermute | solution.py:15
  406.2 30.6 %collective-permute-start.1 = (bf16[1,8,512]{2,1,0:T(8,128)(2,1)S(1)}, bf16[1,8,512]{2,1,0:T(8,128)(2,1)S(1)}, u32[]{:S(2)}, u32[]{:S(2)}) collective-permute-start(bf16[1,8,512]{2,1,0:T(8,128)(2,1)S(1)} %get-tuple-element.754), channel_id=1, source_target_pairs={{8,0},{9,1},{10,2},{11,3},{12,4},{13,5},{14,6},{15,7},{16,8},{17,9... | collective-permute-start | bytes 24584 | tf_op jit(solution)/shard_map/while/body/eval_jaxpr/ppermute | solution.py:15
  409.5 27.4 %collective-permute-start.3 = (bf16[16,1,512]{2,1,0:T(2,128)(2,1)}, bf16[16,1,512]{2,1,0:T(2,128)(2,1)S(1)}, u32[]{:S(2)}, u32[]{:S(2)}) collective-permute-start(bf16[16,1,512]{2,1,0:T(2,128)(2,1)} %get-tuple-element.756), channel_id=1, source_target_pairs={{1,0},{2,1},{3,2},{4,3},{5,4},{6,5},{7,6},{8,7},{9,8},{10,9},{11,1... | collective-permute-start | bytes 49160 | tf_op jit(solution)/shard_map/while/body/eval_jaxpr/ppermute | solution.py:15
  459.0 33.1 %collective-permute-start.9 = (bf16[16,1,1024]{2,1,0:T(2,128)(2,1)S(1)}, bf16[16,1,1024]{2,1,0:T(2,128)(2,1)S(1)}, u32[]{:S(2)}, u32[]{:S(2)}) collective-permute-start(bf16[16,1,1024]{2,1,0:T(2,128)(2,1)S(1)} %get-tuple-element.790), channel_id=1, source_target_pairs={{1,0},{2,1},{3,2},{4,3},{5,4},{6,5},{7,6},{8,7},{9,8},{10,9},{11,1... | collective-permute-start | bytes 98312 | tf_op jit(solution)/shard_map/while/body/eval_jaxpr/ppermute | solution.py:15
  461.7 30.4 %collective-permute-start.10 = (bf16[16,1,1024]{2,1,0:T(2,128)(2,1)S(1)}, bf16[16,1,1024]{2,1,0:T(2,128)(2,1)S(1)}, u32[]{:S(2)}, u32[]{:S(2)}) collective-permute-start(bf16[16,1,1024]{2,1,0:T(2,128)(2,1)S(1)} %get-tuple-element.791), channel_id=1, source_target_pairs={{0,1},{1,2},{2,3},{3,4},{4,5},{5,6},{6,7},{7,8},{8,9},{9,10},{10,1... | collective-permute-start | bytes 98312 | tf_op jit(solution)/shard_map/while/body/eval_jaxpr/ppermute | solution.py:15
  507.6 34.0 %collective-permute-start.9 = (bf16[16,1,1024]{2,1,0:T(2,128)(2,1)S(1)}, bf16[16,1,1024]{2,1,0:T(2,128)(2,1)S(1)}, u32[]{:S(2)}, u32[]{:S(2)}) collective-permute-start(bf16[16,1,1024]{2,1,0:T(2,128)(2,1)S(1)} %get-tuple-element.790), channel_id=1, source_target_pairs={{1,0},{2,1},{3,2},{4,3},{5,4},{6,5},{7,6},{8,7},{9,8},{10,9},{11,1... | collective-permute-start | bytes 98312 | tf_op jit(solution)/shard_map/while/body/eval_jaxpr/ppermute | solution.py:15
  556.9 32.0 %collective-permute-start.9 = (bf16[16,1,1024]{2,1,0:T(2,128)(2,1)S(1)}, bf16[16,1,1024]{2,1,0:T(2,128)(2,1)S(1)}, u32[]{:S(2)}, u32[]{:S(2)}) collective-permute-start(bf16[16,1,1024]{2,1,0:T(2,128)(2,1)S(1)} %get-tuple-element.790), channel_id=1, source_target_pairs={{1,0},{2,1},{3,2},{4,3},{5,4},{6,5},{7,6},{8,7},{9,8},{10,9},{11,1... | collective-permute-start | bytes 98312 | tf_op jit(solution)/shard_map/while/body/eval_jaxpr/ppermute | solution.py:15
  604.2 32.2 %collective-permute-start.9 = (bf16[16,1,1024]{2,1,0:T(2,128)(2,1)S(1)}, bf16[16,1,1024]{2,1,0:T(2,128)(2,1)S(1)}, u32[]{:S(2)}, u32[]{:S(2)}) collective-permute-start(bf16[16,1,1024]{2,1,0:T(2,128)(2,1)S(1)} %get-tuple-element.790), channel_id=1, source_target_pairs={{1,0},{2,1},{3,2},{4,3},{5,4},{6,5},{7,6},{8,7},{9,8},{10,9},{11,1... | collective-permute-start | bytes 98312 | tf_op jit(solution)/shard_map/while/body/eval_jaxpr/ppermute | solution.py:15
  651.7 32.0 %collective-permute-start.9 = (bf16[16,1,1024]{2,1,0:T(2,128)(2,1)S(1)}, bf16[16,1,1024]{2,1,0:T(2,128)(2,1)S(1)}, u32[]{:S(2)}, u32[]{:S(2)}) collective-permute-start(bf16[16,1,1024]{2,1,0:T(2,128)(2,1)S(1)} %get-tuple-element.790), channel_id=1, source_target_pairs={{1,0},{2,1},{3,2},{4,3},{5,4},{6,5},{7,6},{8,7},{9,8},{10,9},{11,1... | collective-permute-start | bytes 98312 | tf_op jit(solution)/shard_map/while/body/eval_jaxpr/ppermute | solution.py:15
  698.9 32.2 %collective-permute-start.9 = (bf16[16,1,1024]{2,1,0:T(2,128)(2,1)S(1)}, bf16[16,1,1024]{2,1,0:T(2,128)(2,1)S(1)}, u32[]{:S(2)}, u32[]{:S(2)}) collective-permute-start(bf16[16,1,1024]{2,1,0:T(2,128)(2,1)S(1)} %get-tuple-element.790), channel_id=1, source_target_pairs={{1,0},{2,1},{3,2},{4,3},{5,4},{6,5},{7,6},{8,7},{9,8},{10,9},{11,1... | collective-permute-start | bytes 98312 | tf_op jit(solution)/shard_map/while/body/eval_jaxpr/ppermute | solution.py:15
  746.4 32.0 %collective-permute-start.9 = (bf16[16,1,1024]{2,1,0:T(2,128)(2,1)S(1)}, bf16[16,1,1024]{2,1,0:T(2,128)(2,1)S(1)}, u32[]{:S(2)}, u32[]{:S(2)}) collective-permute-start(bf16[16,1,1024]{2,1,0:T(2,128)(2,1)S(1)} %get-tuple-element.790), channel_id=1, source_target_pairs={{1,0},{2,1},{3,2},{4,3},{5,4},{6,5},{7,6},{8,7},{9,8},{10,9},{11,1... | collective-permute-start | bytes 98312 | tf_op jit(solution)/shard_map/while/body/eval_jaxpr/ppermute | solution.py:15
  793.7 32.2 %collective-permute-start.9 = (bf16[16,1,1024]{2,1,0:T(2,128)(2,1)S(1)}, bf16[16,1,1024]{2,1,0:T(2,128)(2,1)S(1)}, u32[]{:S(2)}, u32[]{:S(2)}) collective-permute-start(bf16[16,1,1024]{2,1,0:T(2,128)(2,1)S(1)} %get-tuple-element.790), channel_id=1, source_target_pairs={{1,0},{2,1},{3,2},{4,3},{5,4},{6,5},{7,6},{8,7},{9,8},{10,9},{11,1... | collective-permute-start | bytes 98312 | tf_op jit(solution)/shard_map/while/body/eval_jaxpr/ppermute | solution.py:15
  841.2 32.0 %collective-permute-start.9 = (bf16[16,1,1024]{2,1,0:T(2,128)(2,1)S(1)}, bf16[16,1,1024]{2,1,0:T(2,128)(2,1)S(1)}, u32[]{:S(2)}, u32[]{:S(2)}) collective-permute-start(bf16[16,1,1024]{2,1,0:T(2,128)(2,1)S(1)} %get-tuple-element.790), channel_id=1, source_target_pairs={{1,0},{2,1},{3,2},{4,3},{5,4},{6,5},{7,6},{8,7},{9,8},{10,9},{11,1... | collective-permute-start | bytes 98312 | tf_op jit(solution)/shard_map/while/body/eval_jaxpr/ppermute | solution.py:15
  (140 other events, 1749.5 us)
Sparse Core Ops, SparseCore 0:
  898.2 97.6 reduce-scatter.1
where the time goes:
time: 1010 us; the launch traced here: 1000 us
  starting transfers between devices  501 us (50%)
  waiting for transfers between devices  215 us (21%)
  matrix products  107 us (11%)
  other arithmetic  87.6 us (9%)
  local copies, waits for them, and re-layouts  61.8 us (6%)
  loops' own time  18.2 us (2%)
  between operations  14.2 us (1%)
    ppermute x162, starting transfers between devices, shifted(): lax.ppermute(value, axis, [(source, source + steps) for source in range(f...  501 us
    ppermute x162, waiting for transfers between devices, shifted(): lax.ppermute(value, axis, [(source, source + steps) for source in range(f...  117 us
    reduce_scatter x1, waiting for transfers between devices, local(): lax.psum_scatter(lax.dot_general(all_patches, all_gates, (((0,), (0,)), (...  97.8 us
    dot_general x9, matrix products, forward_step(): jnp.dot(patch_rows(padded, tile_rows, tile_cols), kernel, preferred_eleme...  47 us
    dot_general x9, matrix products, backward_step(): jnp.dot(flipped_rows(padded, tile_rows, tile_cols), flipped, preferred_el...  46.9 us
    dynamic_update_slice x54, other arithmetic, store_at(): lax.dynamic_update_index_in_dim(store, jnp.where(is_live, value, previous...  39.9 us
  transfers between devices with their start and end apart: 163, of which 37 were waited for; matrix products, arithmetic and copies ran while one was open for 5% of the time, Pallas kernels for 0%

commit v1 on v0

v1 whole, which is shorter than its diff:
```python
import jax
import jax.numpy as jnp
from jax import lax
from jax.experimental import pallas as pl
from jax.experimental.pallas import tpu as pltpu
from jax.sharding import PartitionSpec as P

MESH = pl.DeviceIdType.MESH
F32 = jnp.float32
BF16 = jnp.bfloat16

C = 256
GC = 1024
STEPS = 6
COLS = 8
ROWS = 16
PIX = COLS * ROWS
ROWS_OUT = 288
HALF = 144
FORGET_SHIFT = 1.0
DIRS = ((-1, -1), (-1, 0), (-1, 1), (0, -1), (0, 1), (1, -1), (1, 0), (1, 1))


def sigmoid(value):
    return 0.5 * jnp.tanh(0.5 * value) + 0.5


def kernel(
    frames, weight, cotangent, hid_out, gin_out, wg_out,
    w, wt, acc, xc, xst, xrim, hs, hst, hrim, st, pst, act, cell, squash, up, gates, gst, grim, sg, pg, gin,
    recurrent, carried, sums, part, from_l, from_r, full_l, full_r, total, from2_l, from2_r, full2_l, full2_r, res, pres,
    w_sem, in_sem, out_sem, xs_send, fr_send, hs_send, gs_send, u_send, ps_send, pg_send,
    xc_recv, x_recv, h_recv, g_recv, u_recv, ps_recv, pg_recv,
    t_send, t_recv, f_send, f_recv, t2_send, t2_recv, f2_send, f2_recv, r_send, r_recv,
):
    layer = lax.axis_index("layer")
    tile = lax.axis_index("tile")
    trow, tcol = tile // 8, lax.rem(tile, 8)
    ypos, core = tcol // 2, lax.rem(tcol, 2)
    mate = tile + 1 - 2 * core

    def there(d):
        dy, dx = DIRS[d]
        found = jnp.bool_(True)
        if dy < 0:
            found = found & (trow > 0)
        if dy > 0:
            found = found & (trow < 3)
        if dx < 0:
            found = found & (tcol > 0)
        if dx > 0:
            found = found & (tcol < 7)
        return found, tile + 8 * dy + dx

    def remote(src, dst, send, recv, to_layer, to_tile):
        return pltpu.make_async_remote_copy(
            src_ref=src, dst_ref=dst, send_sem=send, recv_sem=recv,
            device_id={"layer": to_layer, "tile": to_tile}, device_id_type=MESH,
        )

    def at_ring(along_y, step):
        if along_y:
            return trow * 8 + lax.rem(ypos + step, 4) * 2 + core
        return lax.rem(trow + step, 4) * 8 + tcol

    w_copy = pltpu.make_async_copy(weight, w, w_sem)
    w_copy.start()

    @pl.when(layer == 0)
    def _():
        pltpu.make_async_copy(frames, xc, in_sem).start()

    @pl.when(layer == 3)
    def _():
        pltpu.make_async_copy(cotangent, up, in_sem).start()

    barrier = pltpu.get_barrier_semaphore()
    expected = jnp.int32(0)

    def greet(found, to_layer, to_tile):
        @pl.when(found)
        def _():
            pl.semaphore_signal(barrier, inc=1, device_id={"layer": to_layer, "tile": to_tile}, device_id_type=MESH)

        return found.astype(jnp.int32)

    for d in range(8):
        found, other = there(d)
        expected += greet(found, layer, other)
        expected += greet(found & (layer > 0), layer - 1, other)
        expected += greet(found & (layer < 3), layer + 1, other)
    expected += greet(layer > 0, layer - 1, tile)
    expected += greet(layer < 3, layer + 1, tile)
    for along_y in (True, False):
        for step in (1, 3):
            expected += greet(jnp.bool_(True), layer, at_ring(along_y, step))

    acc[...] = jnp.zeros_like(acc)
    recurrent[...] = jnp.zeros_like(recurrent)
    carried[...] = jnp.zeros_like(carried)
    cell[0] = jnp.zeros((PIX, C), F32)
    st[0, :, :, :, C:] = jnp.zeros((3, COLS + 2, ROWS, C), BF16)
    for d in range(8):
        found, _ = there(d)

        @pl.when(jnp.logical_not(found))
        def _(d=d):
            xrim[d] = jnp.zeros((STEPS, ROWS, C), BF16)
            hrim[d] = jnp.zeros((STEPS, ROWS, C), BF16)
            grim[d] = jnp.zeros((STEPS, ROWS, GC), BF16)

    pl.semaphore_wait(barrier, expected)

    pixel_row = lax.broadcasted_iota(jnp.int32, (ROWS, 1), 0)
    is_top = pixel_row == 0
    is_bottom = pixel_row == ROWS - 1

    def put_centre(dst, lanes, value):
        wide = value.shape[-1]
        dst[0, 1:9, :, lanes] = pltpu.roll(value, 1, 0).astype(BF16).reshape(COLS, ROWS, wide)
        dst[1, 1:9, :, lanes] = value.astype(BF16).reshape(COLS, ROWS, wide)
        dst[2, 1:9, :, lanes] = pltpu.roll(value, PIX - 1, 0).astype(BF16).reshape(COLS, ROWS, wide)

    def put_rim(dst, lanes, rim, t):
        wide = rim.shape[-1]
        top = rim[1, t].astype(F32)[0:8].reshape(COLS, 1, wide)
        bottom = rim[6, t].astype(F32)[0:8].reshape(COLS, 1, wide)
        dst[0, 1:9, :, lanes] = jnp.where(is_top[None], top, dst[0, 1:9, :, lanes].astype(F32)).astype(BF16)
        dst[2, 1:9, :, lanes] = jnp.where(is_bottom[None], bottom, dst[2, 1:9, :, lanes].astype(F32)).astype(BF16)
        for column, side, above, below, at in ((0, 3, 0, 5, 7), (9, 4, 2, 7, 0)):
            value = rim[side, t].astype(F32)
            upper = rim[above, t].astype(F32)[at : at + 1]
            lower = rim[below, t].astype(F32)[at : at + 1]
            dst[0, column, :, lanes] = jnp.where(is_top, upper, pltpu.roll(value, 1, 0)).astype(BF16)
            dst[1, column, :, lanes] = rim[side, t]
            dst[2, column, :, lanes] = jnp.where(is_bottom, lower, pltpu.roll(value, ROWS - 1, 0)).astype(BF16)

    def put_stage(stage, t, lanes, value):
        cut = value.reshape(COLS, ROWS, value.shape[-1])
        for side, at in ((0, 0), (1, ROWS - 1)):
            row = cut[:, at, :]
            stage[t, side, :, lanes] = jnp.concatenate([row, row], axis=0).astype(BF16)

    def rim_source(d, store, stage, t):
        dy, dx = DIRS[d]
        if dy < 0:
            return stage.at[t, 0]
        if dy > 0:
            return stage.at[t, 1]
        return store.at[t, 0 if dx < 0 else COLS - 1]

    def send_rims(store, stage, rim, t, send, recv, to_layer, first):
        for d in range(8):
            found, other = there(d)

            @pl.when(found)
            def _(d=d, other=other):
                copy = remote(
                    rim_source(d, store, stage, t), rim.at[7 - d, t], send.at[d], recv.at[7 - d, t], to_layer, other
                )

                @pl.when(jnp.logical_not(first))
                def _():
                    copy.wait_send()

                copy.start()

    def end_rims(store, stage, rim, send, recv):
        for d in range(8):
            found, other = there(d)

            @pl.when(found)
            def _(d=d, other=other):
                remote(
                    rim_source(d, store, stage, 0), rim.at[7 - d, 0], send.at[d], recv.at[7 - d, 0], layer, other
                ).wait_send()

    def wait_rims(rim, t, send, recv):
        for d in range(8):
            found, other = there(d)

            @pl.when(found)
            def _(d=d, other=other):
                remote(rim.at[d, t], rim.at[d, t], send.at[d], recv.at[d, t], layer, other).wait_recv()

    def turn_weight():
        def one(k, _):
            rows = pl.multiple_of(k * 512, 512)
            wt[pl.ds(pl.multiple_of(k * GC, GC), GC), :] = w[pl.ds(rows, 512), :].T
            return 0

        lax.fori_loop(0, 9, one, 0)

    @pl.when(layer == 0)
    def _():
        pltpu.make_async_copy(frames, xc, in_sem).wait()

        def one(t, _):
            put_stage(xst, t, slice(0, C), xc[t].astype(F32).reshape(PIX, C))
            send_rims(xc, xst, xrim, t, fr_send, x_recv, layer, t == 0)
            return 0

        lax.fori_loop(0, STEPS, one, 0)
        end_rims(xc, xst, xrim, fr_send, x_recv)

    w_copy.wait()

    @pl.when(layer == 3)
    def _():
        pltpu.make_async_copy(cotangent, up, in_sem).wait()
        turn_weight()

    def mate_patches(t):
        return remote(st.at[t], pst.at[t], ps_send, ps_recv.at[t], layer, mate)

    def above_map(t):
        return remote(hs.at[t], xc.at[t], xs_send.at[8], xc_recv.at[t], layer + 1, tile)

    def forward(t, _):
        @pl.when(layer > 0)
        def _():
            remote(xc.at[t], xc.at[t], xs_send.at[8], xc_recv.at[t], layer - 1, tile).wait_recv()

        put_centre(st.at[t], slice(0, C), xc[t].astype(F32).reshape(PIX, C))
        wait_rims(xrim, t, xs_send, x_recv)
        put_rim(st.at[t], slice(0, C), xrim, t)

        @pl.when(t > 0)
        def _():
            wait_rims(hrim, t - 1, hs_send, h_recv)
            put_rim(st.at[t], slice(C, 2 * C), hrim, t - 1)
            mate_patches(t - 1).wait_send()

        mate_patches(t).start()
        patches = jnp.concatenate(
            [st[t, p, q : q + 8].reshape(PIX, 2 * C) for p in range(3) for q in range(3)], axis=1
        )
        sums[...] = jnp.dot(patches, w[...], preferred_element_type=F32)
        in_gate = sigmoid(sums[:, 0:C])
        forget = sigmoid(sums[:, C : 2 * C] + FORGET_SHIFT)
        out_gate = sigmoid(sums[:, 2 * C : 3 * C])
        update = jnp.tanh(sums[:, 3 * C :])
        fresh = forget * cell[t] + in_gate * update
        squashed = jnp.tanh(fresh)
        hidden = out_gate * squashed
        hs[t] = hidden.astype(BF16).reshape(COLS, ROWS, C)
        put_stage(hst, t, slice(0, C), hidden)

        @pl.when(t < STEPS - 1)
        def _():
            send_rims(hs, hst, hrim, t, hs_send, h_recv, layer, t == 0)

        @pl.when(layer < 3)
        def _():
            @pl.when(t > 0)
            def _():
                above_map(t - 1).wait_send()

            above_map(t).start()
            send_rims(hs, hst, xrim, t, xs_send, x_recv, layer + 1, t == 0)

        act[t, :, 0:C] = in_gate
        act[t, :, C : 2 * C] = forget
        act[t, :, 2 * C : 3 * C] = out_gate
        act[t, :, 3 * C :] = update
        cell[t + 1] = fresh
        squash[t] = squashed

        @pl.when(t < STEPS - 1)
        def _():
            put_centre(st.at[t + 1], slice(C, 2 * C), hidden)

        return 0

    lax.fori_loop(0, STEPS, forward, 0)
    mate_patches(STEPS - 1).wait_send()
    end_rims(hs, hst, hrim, hs_send, h_recv)

    hid_copy = pltpu.make_async_copy(hs, hid_out, out_sem.at[0])
    hid_copy.start()

    @pl.when(layer < 3)
    def _():
        turn_weight()
        above_map(STEPS - 1).wait_send()
        end_rims(hs, hst, xrim, xs_send, x_recv)

    mine = pl.ds(pl.multiple_of(core * 512, 512), 512)
    theirs = pl.ds(pl.multiple_of((1 - core) * 512, 512), 512)

    def mate_gates(t):
        return remote(gates.at[t, :, theirs], pg.at[t], pg_send, pg_recv.at[t], layer, mate)

    def weight_terms(t, p, q):
        lhs = jnp.concatenate(
            [st[t, p, q : q + 8].reshape(PIX, 2 * C), pst[t, p, q : q + 8].reshape(PIX, 2 * C)], axis=0
        )
        rhs = jnp.concatenate([gates[t, :, mine], pg[t]], axis=0)
        return lax.dot_general(lhs, rhs, (((0,), (0,)), ((), ())), preferred_element_type=F32)

    def wait_mate(t):
        mate_patches(t).wait_recv()
        mate_gates(t).wait_recv()

    def below_grad(t):
        return remote(gin.at[t], up.at[t], u_send, u_recv.at[t], layer - 1, tile)

    def backward(i, _):
        t = STEPS - 1 - i

        @pl.when(layer < 3)
        def _():
            remote(up.at[t], up.at[t], u_send, u_recv.at[t], layer + 1, tile).wait_recv()

        grad_hidden = up[t].astype(F32).reshape(PIX, C) + recurrent[...]
        in_gate = act[t, :, 0:C]
        forget = act[t, :, C : 2 * C]
        out_gate = act[t, :, 2 * C : 3 * C]
        update = act[t, :, 3 * C :]
        squashed = squash[t]
        grad_cell = grad_hidden * out_gate * (1.0 - squashed * squashed) + carried[...]
        carried[...] = grad_cell * forget
        parts = (
            grad_cell * update * in_gate * (1.0 - in_gate),
            grad_cell * cell[t] * forget * (1.0 - forget),
            grad_hidden * squashed * out_gate * (1.0 - out_gate),
            grad_cell * in_gate * (1.0 - update * update),
        )
        for n, value in enumerate(parts):
            lanes = slice(C * n, C * n + C)
            gates[t, :, lanes] = value.astype(BF16)
            put_stage(gst, t, lanes, value)
            sg[1, 1:9, :, lanes] = value.astype(BF16).reshape(COLS, ROWS, C)
            gst[t, 2, :, lanes] = value[0:ROWS].astype(BF16)
            gst[t, 3, :, lanes] = value[PIX - ROWS :].astype(BF16)
        for d in range(8):
            found, other = there(d)

            @pl.when(found)
            def _(d=d, other=other):
                dy, dx = DIRS[d]
                side = 0 if dy < 0 else 1 if dy > 0 else 2 if dx < 0 else 3
                copy = remote(gst.at[t, side], grim.at[7 - d, t], gs_send.at[d], g_recv.at[7 - d, t], layer, other)

                @pl.when(i > 0)
                def _():
                    copy.wait_send()

                copy.start()

        @pl.when(i > 0)
        def _():
            mate_gates(t + 1).wait_send()

        mate_gates(t).start()
        for n, value in enumerate(parts):
            lanes = slice(C * n, C * n + C)
            sg[0, 1:9, :, lanes] = pltpu.roll(value, 1, 0).astype(BF16).reshape(COLS, ROWS, C)
            sg[2, 1:9, :, lanes] = pltpu.roll(value, PIX - 1, 0).astype(BF16).reshape(COLS, ROWS, C)

        @pl.when(i > 0)
        def _():
            wait_mate(t + 1)
            for p in range(3):
                for q in range(3):
                    k = 3 * p + q
                    acc[512 * k : 512 * k + 512] += weight_terms(t + 1, p, q)

        wait_rims(grim, t, gs_send, g_recv)
        put_rim(sg, slice(0, GC), grim, t)
        patches = jnp.concatenate(
            [sg[2 - p, 2 - q : 10 - q].reshape(PIX, GC) for p in range(3) for q in range(3)], axis=1
        )
        gin[t] = jnp.dot(patches, wt[:, 0:C], preferred_element_type=F32).astype(BF16).reshape(COLS, ROWS, C)

        @pl.when(layer > 0)
        def _():
            @pl.when(i > 0)
            def _():
                below_grad(t + 1).wait_send()

            below_grad(t).start()

        @pl.when(t > 0)
        def _():
            again = jnp.concatenate(
                [sg[2 - p, 2 - q : 10 - q].reshape(PIX, GC) for p in range(3) for q in range(3)], axis=1
            )
            recurrent[...] = jnp.dot(again, wt[:, C:], preferred_element_type=F32)

        return 0

    lax.fori_loop(0, STEPS, backward, 0)
    gin_copy = pltpu.make_async_copy(gin, gin_out, out_sem.at[1])
    gin_copy.start()
    wait_mate(0)
    mate_gates(0).wait_send()
    for p in range(3):
        for q in range(3):
            k = 3 * p + q
            value = (acc[512 * k : 512 * k + 512] + weight_terms(0, p, q)).astype(BF16)
            low = 512 * k
            while low < 512 * k + 512:
                block = low // ROWS_OUT
                high = min(512 * k + 512, ROWS_OUT * (block + 1))
                rows = slice(low - ROWS_OUT * block, high - ROWS_OUT * block)
                z, y = block // 4, block % 4
                part[0, y, z, rows] = value[low - 512 * k : high - 512 * k, 0:256]
                part[1, z, y, rows] = value[low - 512 * k : high - 512 * k, 256:512]
                low = high

    @pl.when(layer > 0)
    def _():
        below_grad(0).wait_send()

    for d in range(8):
        found, other = there(d)

        @pl.when(found)
        def _(d=d, other=other):
            remote(gst.at[0, 0], grim.at[7 - d, 0], gs_send.at[d], g_recv.at[7 - d, 0], layer, other).wait_send()

    def plus(left, right):
        return (left.astype(F32) + right.astype(F32)).astype(BF16)

    def own(n):
        return (ypos, trow) if n == 0 else (trow, ypos)

    rights, lefts = (2, 1), (3, 0)
    sent = []

    def go(copy):
        copy.start()
        sent.append(copy)
        return copy

    def hop(n, first, to_right):
        return at_ring((n == 0) == first, 1 if to_right else 3)

    hand = {}
    full = {}
    for n in range(2):
        a, b = own(n)
        for m in range(2):
            for right in (True, False):
                j = (rights if right else lefts)[m]
                hand[n, m, right] = go(remote(
                    part.at[n, lax.rem(a + 2, 4), lax.rem(b + j, 4)], (from_l if right else from_r).at[n, m],
                    t_send.at[n, m, int(right)], t_recv.at[n, m, int(right)], layer, hop(n, True, right),
                ))

    def send_full(n, j, right):
        a, b = own(n)
        full[n, j, right] = go(remote(
            part.at[n, lax.rem(a + (1 if right else 3), 4), lax.rem(b + j, 4)], (full_l if right else full_r).at[n, j],
            f_send.at[n, j, int(right)], f_recv.at[n, j, int(right)], layer, hop(n, True, right),
        ))

    for m in range(2):
        for n in range(2):
            send_full(n, lefts[m], True)
            send_full(n, rights[m], False)
    for m in range(2):
        for n in range(2):
            a, b = own(n)
            for right in (True, False):
                j = (rights if right else lefts)[m]
                hand[n, m, right].wait_recv()
                to = (n, lax.rem(a + (1 if right else 3), 4), lax.rem(b + j, 4))
                part[to] = plus(part[to], (from_l if right else from_r)[n, m])
                send_full(n, j, right)

    def gather(n, j):
        a, b = own(n)
        full[n, j, True].wait_recv()
        full[n, j, False].wait_recv()
        total[n, j] = (
            part[n, a, lax.rem(b + j, 4)].astype(F32) + full_l[n, j].astype(F32) + full_r[n, j].astype(F32)
        ).astype(BF16)

    upper, lower = pl.ds(0, HALF), pl.ds(HALF, HALF)
    hand2 = {}
    full2 = {}

    def send_full2(n, right, first):
        rows = lower if right == first else upper
        full2[n, right, first] = go(remote(
            total.at[n, 1 if right else 3, rows], (full2_l if right else full2_r).at[n, rows],
            f2_send.at[n, int(right), int(first)], f2_recv.at[n, int(right), int(first)], layer, hop(n, False, right),
        ))

    for n in range(2):
        gather(n, 2)
        for right in (True, False):
            hand2[n, right] = go(remote(
                total.at[n, 2, upper if right else lower], (from2_l if right else from2_r).at[n],
                t2_send.at[n, int(right)], t2_recv.at[n, int(right)], layer, hop(n, False, right),
            ))
    for right in (True, False):
        for n in range(2):
            gather(n, 1 if right else 3)
            send_full2(n, right, True)
    for n in range(2):
        for right in (True, False):
            hand2[n, right].wait_recv()
            at = (n, 1 if right else 3, upper if right else lower)
            total[at] = plus(total[at], (from2_l if right else from2_r)[n])
            send_full2(n, right, False)
    for n in range(2):
        gather(n, 0)
    for n in range(2):
        for right in (True, False):
            for first in (True, False):
                full2[n, right, first].wait_recv()
        res[:, 256 * n : 256 * n + 256] = plus(
            total[n, 0].astype(F32) + full2_l[n].astype(F32), full2_r[n]
        )
    last = go(remote(
        res.at[pl.ds(pl.multiple_of((1 - core) * HALF, HALF), HALF)], pres, r_send, r_recv, layer, mate
    ))
    wg_out[:, mine] = res[pl.ds(pl.multiple_of(core * HALF, HALF), HALF), :].astype(F32)
    last.wait_recv()
    wg_out[:, theirs] = pres[...].astype(F32)
    for copy in sent:
        copy.wait_send()
    hid_copy.wait()
    gin_copy.wait()


def local(frames, weight, cotangent):
    maps = jax.ShapeDtypeStruct((STEPS, COLS, ROWS, C), BF16)
    vmem = pltpu.VMEM
    dma = pltpu.SemaphoreType.DMA
    shape = (STEPS, COLS, ROWS, C)
    block = (ROWS_OUT, 256)
    hidden, grads, weight_grad = pl.pallas_call(
        kernel,
        out_shape=(maps, maps, jax.ShapeDtypeStruct((HALF, GC), F32)),
        in_specs=[pl.BlockSpec(memory_space=pl.ANY)] * 3,
        out_specs=(
            pl.BlockSpec(memory_space=pl.ANY),
            pl.BlockSpec(memory_space=pl.ANY),
            pl.BlockSpec(memory_space=pltpu.VMEM),
        ),
        scratch_shapes=[
            vmem((4608, GC), BF16),
            vmem((9 * GC, 2 * C), BF16),
            vmem((4608, 512), F32),
            vmem(shape, BF16),
            vmem((STEPS, 2, ROWS, C), BF16),
            vmem((8, STEPS, ROWS, C), BF16),
            vmem(shape, BF16),
            vmem((STEPS, 2, ROWS, C), BF16),
            vmem((8, STEPS, ROWS, C), BF16),
            vmem((STEPS, 3, COLS + 2, ROWS, 2 * C), BF16),
            vmem((STEPS, 3, COLS + 2, ROWS, 2 * C), BF16),
            vmem((STEPS, PIX, GC), F32),
            vmem((STEPS + 1, PIX, C), F32),
            vmem((STEPS, PIX, C), F32),
            vmem(shape, BF16),
            vmem((STEPS, PIX, GC), BF16),
            vmem((STEPS, 4, ROWS, GC), BF16),
            vmem((8, STEPS, ROWS, GC), BF16),
            vmem((3, COLS + 2, ROWS, GC), BF16),
            vmem((STEPS, PIX, 512), BF16),
            vmem(shape, BF16),
            vmem((PIX, C), F32),
            vmem((PIX, C), F32),
            vmem((PIX, GC), F32),
            vmem((2, 4, 4) + block, BF16),
            vmem((2, 2) + block, BF16),
            vmem((2, 2) + block, BF16),
            vmem((2, 4) + block, BF16),
            vmem((2, 4) + block, BF16),
            vmem((2, 4) + block, BF16),
            vmem((2, HALF, 256), BF16),
            vmem((2, HALF, 256), BF16),
            vmem((2,) + block, BF16),
            vmem((2,) + block, BF16),
            vmem((ROWS_OUT, 512), BF16),
            vmem((HALF, 512), BF16),
            dma, dma, dma((2,)),
            dma((9,)), dma((8,)), dma((8,)), dma((8,)), dma, dma, dma,
            dma((STEPS,)), dma((8, STEPS)), dma((8, STEPS)), dma((8, STEPS)),
            dma((STEPS,)), dma((STEPS,)), dma((STEPS,)),
            dma((2, 2, 2)), dma((2, 2, 2)), dma((2, 4, 2)), dma((2, 4, 2)),
            dma((2, 2)), dma((2, 2)), dma((2, 2, 2)), dma((2, 2, 2)), dma, dma,
        ],
        compiler_params=pltpu.CompilerParams(
            collective_id=0, has_side_effects=True, vmem_limit_bytes=63 * 2**20
        ),
    )(
        frames[:, 0].transpose(0, 2, 1, 3),
        weight[0],
        cotangent[:, 0].transpose(0, 2, 1, 3),
    )
    hidden = hidden.transpose(0, 2, 1, 3)
    grads = grads.transpose(0, 2, 1, 3)
    return hidden[None, :, None], grads[None, :, None], weight_grad[None]


def solution(mesh):
    in_specs = (
        P(None, "tile", None, None, None),
        P("layer", None, None),
        P(None, "tile", None, None, None),
    )
    out_specs = (
        P("layer", None, "tile", None, None, None),
        P("layer", None, "tile", None, None, None),
        P("layer", "tile", None),
    )
    return jax.shard_map(local, mesh=mesh, in_specs=in_specs, out_specs=out_specs, check_vma=False)
```

time: 1010 us -> 160 us (0.16)
  starting transfers between devices: 501 us -> 0 us
  waiting for transfers between devices: 215 us -> 0 us
  Pallas kernels: 0 us -> 152 us
  matrix products: 107 us -> 0 us
  other arithmetic: 87.6 us -> 0 us
  local copies, waits for them, and re-layouts: 61.8 us -> 7.83 us
  loops' own time: 18.2 us -> 0 us
  between operations: 14.2 us -> 0.64 us
    ppermute x162 -> x0, starting transfers between devices: 501 us -> none  [shifted(): lax.ppermute(value, axis, [(source, source + steps) for source in range(f...]
    pallas_call x0 -> x1, Pallas kernels: none -> 152 us  [local(): pl.pallas_call(kernel, out_shape=(maps, maps, jax.ShapeDtypeStruct((HALF,...]
    ppermute x162 -> x0, waiting for transfers between devices: 117 us -> none  [shifted(): lax.ppermute(value, axis, [(source, source + steps) for source in range(f...]
    dot_general x19 -> x0, matrix products: 107 us -> none  [the longest x9 47 us: forward_step(): jnp.dot(patch_rows(padded, tile_rows, tile_cols), kernel, preferred_eleme...]
    reduce_scatter x1 -> x0, waiting for transfers between devices: 97.8 us -> none  [local(): lax.psum_scatter(lax.dot_general(all_patches, all_gates, (((0,), (0,)), (...]
    dynamic_update_slice x54 -> x0, other arithmetic: 39.9 us -> none  [store_at(): lax.dynamic_update_index_in_dim(store, jnp.where(is_live, value, previous...]
    select_n x135 -> x0, other arithmetic: 25.7 us -> none  [the longest x108 8.97 us: extend(): arrived = jnp.where(column == border, jnp.zeros_like(arrived), arrived)]
    dynamic_slice x36 -> x0, local copies, waits for them, and re-layouts: 23.9 us -> none  [the longest x18 16.2 us: local(): lax.scan(forward_step, start_state, jnp.arange(wave_count, dtype=jnp.int32))]
  transfers between devices with their start and end apart: 163 -> 0, of which waited for: 37 -> 0; matrix products, arithmetic and copies ran while one was open for 5% -> 0% of each run, Pallas kernels for 0% -> 0%
where the time goes in v1:
time: 160 us
  Pallas kernels  152 us (95%)
  local copies, waits for them, and re-layouts  7.83 us (5%)
    pallas_call x1, Pallas kernels, local(): pl.pallas_call(kernel, out_shape=(maps, maps, jax.ShapeDtypeStruct((HALF,...  152 us
    unnamed x3, local copies, waits for them, and re-layouts  5.66 us

profile of v1, /device:TPU:1, one launch (start us, length us, event | category | flops | bytes accessed | tf_op | source)
XLA Modules:
  0.0 160.1 jit_solution(9567775041733968595)
XLA Ops:
  0.6 2.2 %copy_bitcast_fusion = (bf16[6,8,16,256]{3,2,1,0:T(8,128)(2,1)}, bf16[6,8,16,256]{3,2,1,0:T(8,128)(2,1)}) fusion(bf16[6,1,16,8,256]{4,3,2,1,0:T(8,128)(2,1)} %param.5, bf16[6,1,16,8,256]{4,3,2,1,0:T(8,128)(2,1)} %param.3), kind=kLoop, calls=%fused_computation | loop fusion | bytes 1572864 | tf_op jit(solution)/shard_map/transpose | solution.py:595
  2.8 151.6 %shard_map.58 = (bf16[6,8,16,256]{3,2,1,0:T(8,128)(2,1)}, bf16[6,8,16,256]{3,2,1,0:T(8,128)(2,1)}, f32[144,1024]{1,0:T(8,128)}) custom-call(bf16[6,8,16,256]{3,2,1,0:T(8,128)(2,1)} %get-tuple-element.13.frames, bf16[4608,1024]{1,0:T(8,128)(2,1)} %bitcast.16, bf16[6,8,16,256]{3,2,1,0:T(8,128)(2,1)} %get-tuple-element.12.cotangent), custom_call_target="tpu_custom_call" | custom-call | tf_op jit(solution)/shard_map/pallas_call | solution.py:536
  154.4 1.9 %copy.8 = bf16[1,6,1,16,8,256]{5,4,3,2,1,0:T(8,128)(2,1)} copy(bf16[1,6,1,16,8,256]{5,3,4,1,2,0:T(8,128)(2,1)} %bitcast.19) | data formatting | bytes 786432
  156.3 1.9 %copy.9 = bf16[1,6,1,16,8,256]{5,4,3,2,1,0:T(8,128)(2,1)} copy(bf16[1,6,1,16,8,256]{5,3,4,1,2,0:T(8,128)(2,1)} %bitcast.18) | data formatting | bytes 786432
  158.1 1.9 %copy.13 = f32[1,144,1024]{2,1,0:T(8,128)} copy(f32[1,144,1024]{2,1,0:T(8,128)} %bitcast.17) | data formatting | bytes 1179648

commit v2 on v1

--- a/solution.py
+++ b/solution.py
@@ -27,10 +27,11 @@
 
 def kernel(
     frames, weight, cotangent, hid_out, gin_out, wg_out,
-    w, wt, acc, xc, xst, xrim, hs, hst, hrim, st, pst, act, cell, squash, up, gates, gst, grim, sg, pg, gin,
+    w, wt, acc, xc, xst, xrim, hs, hst, hrim, st, pst, act, cell, squash, up, gates, pg, hrow, gin,
+    rrim, urim, grim, rstage, gstage, gown, gsum, spread,
     recurrent, carried, sums, part, from_l, from_r, full_l, full_r, total, from2_l, from2_r, full2_l, full2_r, res, pres,
-    w_sem, in_sem, out_sem, xs_send, fr_send, hs_send, gs_send, u_send, ps_send, pg_send,
-    xc_recv, x_recv, h_recv, g_recv, u_recv, ps_recv, pg_recv,
+    w_sem, in_sem, out_sem, xs_send, fr_send, hs_send, rs_send, us_send, gs_send, ps_send, pg_send,
+    xc_recv, x_recv, h_recv, r_recv_rim, u_recv_rim, g_recv_rim, u_recv, ps_recv, pg_recv,
     t_send, t_recv, f_send, f_recv, t2_send, t2_recv, f2_send, f2_recv, r_send, r_recv,
 ):
     layer = lax.axis_index("layer")
@@ -63,16 +64,17 @@
             return trow * 8 + lax.rem(ypos + step, 4) * 2 + core
         return lax.rem(trow + step, 4) * 8 + tcol
 
-    w_copy = pltpu.make_async_copy(weight, w, w_sem)
-    w_copy.start()
-
     @pl.when(layer == 0)
     def _():
-        pltpu.make_async_copy(frames, xc, in_sem).start()
+        pltpu.make_async_copy(frames, gin, in_sem).start()
 
     @pl.when(layer == 3)
     def _():
-        pltpu.make_async_copy(cotangent, up, in_sem).start()
+        pltpu.make_async_copy(cotangent, gin, in_sem).start()
+
+    w_copies = [pltpu.make_async_copy(weight.at[:, n], w.at[n], w_sem.at[n]) for n in range(2)]
+    for copy in w_copies:
+        copy.start()
 
     barrier = pltpu.get_barrier_semaphore()
     expected = jnp.int32(0)
@@ -99,7 +101,7 @@
     recurrent[...] = jnp.zeros_like(recurrent)
     carried[...] = jnp.zeros_like(carried)
     cell[0] = jnp.zeros((PIX, C), F32)
-    st[0, :, :, :, C:] = jnp.zeros((3, COLS + 2, ROWS, C), BF16)
+    st[0, 1] = jnp.zeros((3, COLS + 2, ROWS, C), BF16)
     for d in range(8):
         found, _ = there(d)
 
@@ -107,7 +109,9 @@
         def _(d=d):
             xrim[d] = jnp.zeros((STEPS, ROWS, C), BF16)
             hrim[d] = jnp.zeros((STEPS, ROWS, C), BF16)
-            grim[d] = jnp.zeros((STEPS, ROWS, GC), BF16)
+            rrim[d] = jnp.zeros((STEPS, ROWS, C), F32)
+            urim[d] = jnp.zeros((STEPS, ROWS, C), F32)
+            grim[d] = jnp.zeros((STEPS, ROWS, C), F32)
 
     pl.semaphore_wait(barrier, expected)
 
@@ -115,31 +119,46 @@
     is_top = pixel_row == 0
     is_bottom = pixel_row == ROWS - 1
 
-    def put_centre(dst, lanes, value):
-        wide = value.shape[-1]
-        dst[0, 1:9, :, lanes] = pltpu.roll(value, 1, 0).astype(BF16).reshape(COLS, ROWS, wide)
-        dst[1, 1:9, :, lanes] = value.astype(BF16).reshape(COLS, ROWS, wide)
-        dst[2, 1:9, :, lanes] = pltpu.roll(value, PIX - 1, 0).astype(BF16).reshape(COLS, ROWS, wide)
-
-    def put_rim(dst, lanes, rim, t):
-        wide = rim.shape[-1]
-        top = rim[1, t].astype(F32)[0:8].reshape(COLS, 1, wide)
-        bottom = rim[6, t].astype(F32)[0:8].reshape(COLS, 1, wide)
-        dst[0, 1:9, :, lanes] = jnp.where(is_top[None], top, dst[0, 1:9, :, lanes].astype(F32)).astype(BF16)
-        dst[2, 1:9, :, lanes] = jnp.where(is_bottom[None], bottom, dst[2, 1:9, :, lanes].astype(F32)).astype(BF16)
+    def put_centre(dst, value):
+        dst[0, 1:9] = pltpu.roll(value, 1, 0).astype(BF16).reshape(COLS, ROWS, C)
+        dst[1, 1:9] = value.astype(BF16).reshape(COLS, ROWS, C)
+        dst[2, 1:9] = pltpu.roll(value, PIX - 1, 0).astype(BF16).reshape(COLS, ROWS, C)
+
+    def put_rim(dst, rim, t):
+        top = rim[1, t].astype(F32)[0:8].reshape(COLS, 1, C)
+        bottom = rim[6, t].astype(F32)[0:8].reshape(COLS, 1, C)
+        dst[0, 1:9] = jnp.where(is_top[None], top, dst[0, 1:9].astype(F32)).astype(BF16)
+        dst[2, 1:9] = jnp.where(is_bottom[None], bottom, dst[2, 1:9].astype(F32)).astype(BF16)
         for column, side, above, below, at in ((0, 3, 0, 5, 7), (9, 4, 2, 7, 0)):
             value = rim[side, t].astype(F32)
             upper = rim[above, t].astype(F32)[at : at + 1]
             lower = rim[below, t].astype(F32)[at : at + 1]
-            dst[0, column, :, lanes] = jnp.where(is_top, upper, pltpu.roll(value, 1, 0)).astype(BF16)
-            dst[1, column, :, lanes] = rim[side, t]
-            dst[2, column, :, lanes] = jnp.where(is_bottom, lower, pltpu.roll(value, ROWS - 1, 0)).astype(BF16)
-
-    def put_stage(stage, t, lanes, value):
-        cut = value.reshape(COLS, ROWS, value.shape[-1])
+            dst[0, column] = jnp.where(is_top, upper, pltpu.roll(value, 1, 0)).astype(BF16)
+            dst[1, column] = rim[side, t]
+            dst[2, column] = jnp.where(is_bottom, lower, pltpu.roll(value, ROWS - 1, 0)).astype(BF16)
+
+    def put_stage(stage, t, value):
+        cut = value.reshape(COLS, ROWS, C)
         for side, at in ((0, 0), (1, ROWS - 1)):
             row = cut[:, at, :]
-            stage[t, side, :, lanes] = jnp.concatenate([row, row], axis=0).astype(BF16)
+            stage[t, side] = jnp.concatenate([row, row], axis=0).astype(BF16)
+
+    def add_rims(value, rim, t):
+        cut = value.reshape(COLS, ROWS, C)
+        cut = cut + jnp.where(is_top[None], rim[1, t, 0:8].reshape(COLS, 1, C), 0.0)
+        cut = cut + jnp.where(is_bottom[None], rim[6, t, 0:8].reshape(COLS, 1, C), 0.0)
+        sides = []
+        for side, above, below in ((3, 0, 5), (4, 2, 7)):
+            column = rim[side, t] + jnp.where(is_top, rim[above, t, 0:1], 0.0)
+            sides.append((column + jnp.where(is_bottom, rim[below, t, 0:1], 0.0))[None])
+        cut = jnp.concatenate([cut[0:1] + sides[0], cut[1:7], cut[7:8] + sides[1]], axis=0)
+        return cut.reshape(PIX, C)
+
+    def by_columns(value):
+        return jnp.transpose(value.astype(F32).reshape(ROWS, COLS, C), (1, 0, 2))
+
+    def by_rows(value):
+        return jnp.transpose(value.reshape(COLS, ROWS, C), (1, 0, 2)).reshape(PIX, C).astype(BF16)
 
     def rim_source(d, store, stage, t):
         dy, dx = DIRS[d]
@@ -185,29 +204,38 @@
 
     def turn_weight():
         def one(k, _):
-            rows = pl.multiple_of(k * 512, 512)
-            wt[pl.ds(pl.multiple_of(k * GC, GC), GC), :] = w[pl.ds(rows, 512), :].T
+            for n in range(2):
+                wt[n, k] = w[n, k].T
             return 0
 
         lax.fori_loop(0, 9, one, 0)
 
     @pl.when(layer == 0)
     def _():
-        pltpu.make_async_copy(frames, xc, in_sem).wait()
+        pltpu.make_async_copy(frames, gin, in_sem).wait()
 
         def one(t, _):
-            put_stage(xst, t, slice(0, C), xc[t].astype(F32).reshape(PIX, C))
+            value = by_columns(gin[t])
+            xc[t] = value.astype(BF16)
+            put_stage(xst, t, value.reshape(PIX, C))
             send_rims(xc, xst, xrim, t, fr_send, x_recv, layer, t == 0)
             return 0
 
         lax.fori_loop(0, STEPS, one, 0)
         end_rims(xc, xst, xrim, fr_send, x_recv)
 
-    w_copy.wait()
+    for copy in w_copies:
+        copy.wait()
 
     @pl.when(layer == 3)
     def _():
-        pltpu.make_async_copy(cotangent, up, in_sem).wait()
+        pltpu.make_async_copy(cotangent, gin, in_sem).wait()
+
+        def one(t, _):
+            up[t] = by_columns(gin[t]).astype(BF16)
+            return 0
+
+        lax.fori_loop(0, STEPS, one, 0)
         turn_weight()
 
     def mate_patches(t):
@@ -216,26 +244,27 @@
     def above_map(t):
         return remote(hs.at[t], xc.at[t], xs_send.at[8], xc_recv.at[t], layer + 1, tile)
 
+    def patches(t, n):
+        taps = [st[t, n, p, q : q + 8].reshape(PIX, C) for p in range(3) for q in range(3)]
+        return jnp.concatenate(taps, axis=1)
+
     def forward(t, _):
         @pl.when(layer > 0)
         def _():
             remote(xc.at[t], xc.at[t], xs_send.at[8], xc_recv.at[t], layer - 1, tile).wait_recv()
 
-        put_centre(st.at[t], slice(0, C), xc[t].astype(F32).reshape(PIX, C))
+        put_centre(st.at[t, 0], xc[t].astype(F32).reshape(PIX, C))
         wait_rims(xrim, t, xs_send, x_recv)
-        put_rim(st.at[t], slice(0, C), xrim, t)
+        put_rim(st.at[t, 0], xrim, t)
+        sums[...] = jnp.dot(patches(t, 0), w[0].reshape(9 * C, GC), preferred_element_type=F32)
 
         @pl.when(t > 0)
         def _():
             wait_rims(hrim, t - 1, hs_send, h_recv)
-            put_rim(st.at[t], slice(C, 2 * C), hrim, t - 1)
+            put_rim(st.at[t, 1], hrim, t - 1)
             mate_patches(t - 1).wait_send()
-
-        mate_patches(t).start()
-        patches = jnp.concatenate(
-            [st[t, p, q : q + 8].reshape(PIX, 2 * C) for p in range(3) for q in range(3)], axis=1
-        )
-        sums[...] = jnp.dot(patches, w[...], preferred_element_type=F32)
+            sums[...] += jnp.dot(patches(t, 1), w[1].reshape(9 * C, GC), preferred_element_type=F32)
+
         in_gate = sigmoid(sums[:, 0:C])
         forget = sigmoid(sums[:, C : 2 * C] + FORGET_SHIFT)
         out_gate = sigmoid(sums[:, 2 * C : 3 * C])
@@ -244,7 +273,7 @@
         squashed = jnp.tanh(fresh)
         hidden = out_gate * squashed
         hs[t] = hidden.astype(BF16).reshape(COLS, ROWS, C)
-        put_stage(hst, t, slice(0, C), hidden)
+        put_stage(hst, t, hidden)
 
         @pl.when(t < STEPS - 1)
         def _():
@@ -259,16 +288,18 @@
             above_map(t).start()
             send_rims(hs, hst, xrim, t, xs_send, x_recv, layer + 1, t == 0)
 
+        mate_patches(t).start()
         act[t, :, 0:C] = in_gate
         act[t, :, C : 2 * C] = forget
         act[t, :, 2 * C : 3 * C] = out_gate
         act[t, :, 3 * C :] = update
         cell[t + 1] = fresh
         squash[t] = squashed
+        hrow[t] = by_rows(hidden)
 
         @pl.when(t < STEPS - 1)
         def _():
-            put_centre(st.at[t + 1], slice(C, 2 * C), hidden)
+            put_centre(st.at[t + 1, 1], hidden)
 
         return 0
 
@@ -276,7 +307,7 @@
     mate_patches(STEPS - 1).wait_send()
     end_rims(hs, hst, hrim, hs_send, h_recv)
 
-    hid_copy = pltpu.make_async_copy(hs, hid_out, out_sem.at[0])
+    hid_copy = pltpu.make_async_copy(hrow, hid_out, out_sem.at[0])
     hid_copy.start()
 
     @pl.when(layer < 3)
@@ -291,9 +322,9 @@
     def mate_gates(t):
         return remote(gates.at[t, :, theirs], pg.at[t], pg_send, pg_recv.at[t], layer, mate)
 
-    def weight_terms(t, p, q):
+    def weight_terms(t, n, p, q):
         lhs = jnp.concatenate(
-            [st[t, p, q : q + 8].reshape(PIX, 2 * C), pst[t, p, q : q + 8].reshape(PIX, 2 * C)], axis=0
+            [st[t, n, p, q : q + 8].reshape(PIX, C), pst[t, n, p, q : q + 8].reshape(PIX, C)], axis=0
         )
         rhs = jnp.concatenate([gates[t, :, mine], pg[t]], axis=0)
         return lax.dot_general(lhs, rhs, (((0,), (0,)), ((), ())), preferred_element_type=F32)
@@ -303,16 +334,86 @@
         mate_gates(t).wait_recv()
 
     def below_grad(t):
-        return remote(gin.at[t], up.at[t], u_send, u_recv.at[t], layer - 1, tile)
+        return remote(gown.at[t], up.at[t], us_send.at[8], u_recv.at[t], layer - 1, tile)
+
+    def spread_out(t, n, stage):
+        for p in range(3):
+            for q in range(3):
+                term = jnp.dot(gates[t], wt[n, 3 * p + q], preferred_element_type=F32)
+                if q == 0:
+                    spread[p, 0:PIX] = term
+                    spread[p, PIX:] = jnp.zeros((2 * ROWS, C), F32)
+                else:
+                    spread[p, ROWS * q : ROWS * q + PIX] += term
+        row = lax.rem(lax.broadcasted_iota(jnp.int32, (PIX + 2 * ROWS, 1), 0), ROWS)
+        upper, lower = spread[0], spread[2]
+        centre = spread[1] + jnp.where(row == ROWS - 1, 0.0, pltpu.roll(upper, PIX + 2 * ROWS - 1, 0))
+        centre = centre + jnp.where(row == 0, 0.0, pltpu.roll(lower, 1, 0))
+        stage[1, 0:8] = upper.reshape(COLS + 2, ROWS, C)[1:9, 0, :]
+        stage[6, 0:8] = lower.reshape(COLS + 2, ROWS, C)[1:9, ROWS - 1, :]
+        stage[3] = centre[0:ROWS]
+        stage[4] = centre[PIX + ROWS :]
+        for d, source, at in ((0, upper, 0), (2, upper, PIX + ROWS), (5, lower, ROWS - 1), (7, lower, PIX + 2 * ROWS - 1)):
+            stage[d, 0:8] = jnp.broadcast_to(source[at : at + 1], (8, C))
+        return centre[ROWS : PIX + ROWS]
+
+    def rim_copies(stage, rim, t, send, recv, to_layer, act_on):
+        for d in range(8):
+            found, other = there(d)
+            rows = pl.ds(0, ROWS if d in (3, 4) else 8)
+
+            @pl.when(found)
+            def _(d=d, other=other, rows=rows):
+                act_on(remote(
+                    stage.at[d, rows], rim.at[7 - d, t, rows], send.at[d], recv.at[7 - d, t], to_layer, other
+                ))
+
+    def rim_arrivals(rim, t, send, recv):
+        for d in range(8):
+            found, other = there(d)
+            rows = pl.ds(0, ROWS if d in (3, 4) else 8)
+
+            @pl.when(found)
+            def _(d=d, other=other, rows=rows):
+                here = rim.at[d, t, rows]
+                remote(here, here, send.at[d], recv.at[d, t], layer, other).wait_recv()
+
+    def begin(copy):
+        copy.start()
+
+    def settle(copy):
+        copy.wait_send()
+
+    def settle_inputs(t):
+        rim_copies(gstage, grim, t, gs_send, g_recv_rim, layer, settle)
+
+        @pl.when(layer > 0)
+        def _():
+            below_grad(t).wait_send()
+            rim_copies(gstage, urim, t, us_send, u_recv_rim, layer - 1, settle)
+
+    def finish_inputs(t):
+        rim_arrivals(grim, t, gs_send, g_recv_rim)
+        gin[t] = by_rows(add_rims(gsum[t], grim, t))
+
+    @pl.when(layer == 3)
+    def _():
+        urim[...] = jnp.zeros_like(urim)
 
     def backward(i, _):
         t = STEPS - 1 - i
 
+        @pl.when(i > 0)
+        def _():
+            rim_arrivals(rrim, t + 1, rs_send, r_recv_rim)
+            recurrent[...] = add_rims(recurrent[...], rrim, t + 1)
+
         @pl.when(layer < 3)
         def _():
-            remote(up.at[t], up.at[t], u_send, u_recv.at[t], layer + 1, tile).wait_recv()
-
-        grad_hidden = up[t].astype(F32).reshape(PIX, C) + recurrent[...]
+            remote(up.at[t], up.at[t], us_send.at[8], u_recv.at[t], layer + 1, tile).wait_recv()
+            rim_arrivals(urim, t, us_send, u_recv_rim)
+
+        grad_hidden = add_rims(up[t].astype(F32).reshape(PIX, C) + recurrent[...], urim, t)
         in_gate = act[t, :, 0:C]
         forget = act[t, :, C : 2 * C]
         out_gate = act[t, :, 2 * C : 3 * C]
@@ -320,105 +421,71 @@
         squashed = squash[t]
         grad_cell = grad_hidden * out_gate * (1.0 - squashed * squashed) + carried[...]
         carried[...] = grad_cell * forget
-        parts = (
-            grad_cell * update * in_gate * (1.0 - in_gate),
-            grad_cell * cell[t] * forget * (1.0 - forget),
-            grad_hidden * squashed * out_gate * (1.0 - out_gate),
-            grad_cell * in_gate * (1.0 - update * update),
-        )
-        for n, value in enumerate(parts):
-            lanes = slice(C * n, C * n + C)
-            gates[t, :, lanes] = value.astype(BF16)
-            put_stage(gst, t, lanes, value)
-            sg[1, 1:9, :, lanes] = value.astype(BF16).reshape(COLS, ROWS, C)
-            gst[t, 2, :, lanes] = value[0:ROWS].astype(BF16)
-            gst[t, 3, :, lanes] = value[PIX - ROWS :].astype(BF16)
-        for d in range(8):
-            found, other = there(d)
-
-            @pl.when(found)
-            def _(d=d, other=other):
-                dy, dx = DIRS[d]
-                side = 0 if dy < 0 else 1 if dy > 0 else 2 if dx < 0 else 3
-                copy = remote(gst.at[t, side], grim.at[7 - d, t], gs_send.at[d], g_recv.at[7 - d, t], layer, other)
-
-                @pl.when(i > 0)
-                def _():
-                    copy.wait_send()
-
-                copy.start()
+        gates[t, :, 0:C] = (grad_cell * update * in_gate * (1.0 - in_gate)).astype(BF16)
+        gates[t, :, C : 2 * C] = (grad_cell * cell[t] * forget * (1.0 - forget)).astype(BF16)
+        gates[t, :, 2 * C : 3 * C] = (grad_hidden * squashed * out_gate * (1.0 - out_gate)).astype(BF16)
+        gates[t, :, 3 * C :] = (grad_cell * in_gate * (1.0 - update * update)).astype(BF16)
 
         @pl.when(i > 0)
         def _():
             mate_gates(t + 1).wait_send()
 
         mate_gates(t).start()
-        for n, value in enumerate(parts):
-            lanes = slice(C * n, C * n + C)
-            sg[0, 1:9, :, lanes] = pltpu.roll(value, 1, 0).astype(BF16).reshape(COLS, ROWS, C)
-            sg[2, 1:9, :, lanes] = pltpu.roll(value, PIX - 1, 0).astype(BF16).reshape(COLS, ROWS, C)
+
+        @pl.when(t > 0)
+        def _():
+            @pl.when(i > 0)
+            def _():
+                rim_copies(rstage, rrim, t + 1, rs_send, r_recv_rim, layer, settle)
+
+            recurrent[...] = spread_out(t, 1, rstage)
+            rim_copies(rstage, rrim, t, rs_send, r_recv_rim, layer, begin)
+
+        @pl.when(i > 0)
+        def _():
+            settle_inputs(t + 1)
+
+        own = spread_out(t, 0, gstage)
+        gown[t] = own.astype(BF16).reshape(COLS, ROWS, C)
+
+        @pl.when(layer > 0)
+        def _():
+            below_grad(t).start()
+            rim_copies(gstage, urim, t, us_send, u_recv_rim, layer - 1, begin)
+
+        rim_copies(gstage, grim, t, gs_send, g_recv_rim, layer, begin)
+        gsum[t] = own
 
         @pl.when(i > 0)
         def _():
             wait_mate(t + 1)
             for p in range(3):
                 for q in range(3):
-                    k = 3 * p + q
-                    acc[512 * k : 512 * k + 512] += weight_terms(t + 1, p, q)
-
-        wait_rims(grim, t, gs_send, g_recv)
-        put_rim(sg, slice(0, GC), grim, t)
-        patches = jnp.concatenate(
-            [sg[2 - p, 2 - q : 10 - q].reshape(PIX, GC) for p in range(3) for q in range(3)], axis=1
-        )
-        gin[t] = jnp.dot(patches, wt[:, 0:C], preferred_element_type=F32).astype(BF16).reshape(COLS, ROWS, C)
-
-        @pl.when(layer > 0)
-        def _():
-            @pl.when(i > 0)
-            def _():
-                below_grad(t + 1).wait_send()
-
-            below_grad(t).start()
-
-        @pl.when(t > 0)
-        def _():
-            again = jnp.concatenate(
-                [sg[2 - p, 2 - q : 10 - q].reshape(PIX, GC) for p in range(3) for q in range(3)], axis=1
-            )
-            recurrent[...] = jnp.dot(again, wt[:, C:], preferred_element_type=F32)
+                    for n in range(2):
+                        low = 512 * (3 * p + q) + C * n
+                        acc[low : low + C] += weight_terms(t + 1, n, p, q)
+            finish_inputs(t + 1)
 
         return 0
 
     lax.fori_loop(0, STEPS, backward, 0)
-    gin_copy = pltpu.make_async_copy(gin, gin_out, out_sem.at[1])
-    gin_copy.start()
+    rim_copies(rstage, rrim, 1, rs_send, r_recv_rim, layer, settle)
     wait_mate(0)
     mate_gates(0).wait_send()
     for p in range(3):
         for q in range(3):
-            k = 3 * p + q
-            value = (acc[512 * k : 512 * k + 512] + weight_terms(0, p, q)).astype(BF16)
-            low = 512 * k
-            while low < 512 * k + 512:
-                block = low // ROWS_OUT
-                high = min(512 * k + 512, ROWS_OUT * (block + 1))
-                rows = slice(low - ROWS_OUT * block, high - ROWS_OUT * block)
-                z, y = block // 4, block % 4
-                part[0, y, z, rows] = value[low - 512 * k : high - 512 * k, 0:256]
-                part[1, z, y, rows] = value[low - 512 * k : high - 512 * k, 256:512]
-                low = high
-
-    @pl.when(layer > 0)
-    def _():
-        below_grad(0).wait_send()
-
-    for d in range(8):
-        found, other = there(d)
-
-        @pl.when(found)
-        def _(d=d, other=other):
-            remote(gst.at[0, 0], grim.at[7 - d, 0], gs_send.at[d], g_recv.at[7 - d, 0], layer, other).wait_send()
+            for n in range(2):
+                start = 512 * (3 * p + q) + C * n
+                value = (acc[start : start + C] + weight_terms(0, n, p, q)).astype(BF16)
+                low = start
+                while low < start + C:
+                    block = low // ROWS_OUT
+                    high = min(start + C, ROWS_OUT * (block + 1))
+                    rows = slice(low - ROWS_OUT * block, high - ROWS_OUT * block)
+                    z, y = block // 4, block % 4
+                    part[0, y, z, rows] = value[low - start : high - start, 0:256]
+                    part[1, z, y, rows] = value[low - start : high - start, 256:512]
+                    low = high
 
     def plus(left, right):
         return (left.astype(F32) + right.astype(F32)).astype(BF16)
@@ -460,6 +527,10 @@
         for n in range(2):
             send_full(n, lefts[m], True)
             send_full(n, rights[m], False)
+    finish_inputs(0)
+    gin_copy = pltpu.make_async_copy(gin, gin_out, out_sem.at[1])
+    gin_copy.start()
+    settle_inputs(0)
     for m in range(2):
         for n in range(2):
             a, b = own(n)
@@ -527,8 +598,16 @@
     gin_copy.wait()
 
 
+def copy_out(a, b, c, a_out, b_out, c_out, sem):
+    copies = [pltpu.make_async_copy(*pair, sem.at[n]) for n, pair in enumerate(((a, a_out), (b, b_out), (c, c_out)))]
+    for copy in copies:
+        copy.start()
+    for copy in copies:
+        copy.wait()
+
+
 def local(frames, weight, cotangent):
-    maps = jax.ShapeDtypeStruct((STEPS, COLS, ROWS, C), BF16)
+    maps = jax.ShapeDtypeStruct((STEPS, PIX, C), BF16)
     vmem = pltpu.VMEM
     dma = pltpu.SemaphoreType.DMA
     shape = (STEPS, COLS, ROWS, C)
@@ -543,8 +622,8 @@
             pl.BlockSpec(memory_space=pltpu.VMEM),
         ),
         scratch_shapes=[
-            vmem((4608, GC), BF16),
-            vmem((9 * GC, 2 * C), BF16),
+            vmem((2, 9, C, GC), BF16),
+            vmem((2, 9, GC, C), BF16),
             vmem((4608, 512), F32),
             vmem(shape, BF16),
             vmem((STEPS, 2, ROWS, C), BF16),
@@ -552,18 +631,24 @@
             vmem(shape, BF16),
             vmem((STEPS, 2, ROWS, C), BF16),
             vmem((8, STEPS, ROWS, C), BF16),
-            vmem((STEPS, 3, COLS + 2, ROWS, 2 * C), BF16),
-            vmem((STEPS, 3, COLS + 2, ROWS, 2 * C), BF16),
+            vmem((STEPS, 2, 3, COLS + 2, ROWS, C), BF16),
+            vmem((STEPS, 2, 3, COLS + 2, ROWS, C), BF16),
             vmem((STEPS, PIX, GC), F32),
             vmem((STEPS + 1, PIX, C), F32),
             vmem((STEPS, PIX, C), F32),
             vmem(shape, BF16),
             vmem((STEPS, PIX, GC), BF16),
-            vmem((STEPS, 4, ROWS, GC), BF16),
-            vmem((8, STEPS, ROWS, GC), BF16),
-            vmem((3, COLS + 2, ROWS, GC), BF16),
             vmem((STEPS, PIX, 512), BF16),
+            vmem((STEPS, PIX, C), BF16),
+            vmem((STEPS, PIX, C), BF16),
+            vmem((8, STEPS, ROWS, C), F32),
+            vmem((8, STEPS, ROWS, C), F32),
+            vmem((8, STEPS, ROWS, C), F32),
+            vmem((8, ROWS, C), F32),
+            vmem((8, ROWS, C), F32),
             vmem(shape, BF16),
+            vmem((STEPS, PIX, C), F32),
+            vmem((3, PIX + 2 * ROWS, C), F32),
             vmem((PIX, C), F32),
             vmem((PIX, C), F32),
             vmem((PIX, GC), F32),
@@ -579,9 +664,10 @@
             vmem((2,) + block, BF16),
             vmem((ROWS_OUT, 512), BF16),
             vmem((HALF, 512), BF16),
-            dma, dma, dma((2,)),
-            dma((9,)), dma((8,)), dma((8,)), dma((8,)), dma, dma, dma,
-            dma((STEPS,)), dma((8, STEPS)), dma((8, STEPS)), dma((8, STEPS)),
+            dma((2,)), dma, dma((2,)),
+            dma((9,)), dma((8,)), dma((8,)), dma((8,)), dma((9,)), dma((8,)), dma, dma,
+            dma((STEPS,)), dma((8, STEPS)), dma((8, STEPS)),
+            dma((8, STEPS)), dma((8, STEPS)), dma((8, STEPS)),
             dma((STEPS,)), dma((STEPS,)), dma((STEPS,)),
             dma((2, 2, 2)), dma((2, 2, 2)), dma((2, 4, 2)), dma((2, 4, 2)),
             dma((2, 2)), dma((2, 2)), dma((2, 2, 2)), dma((2, 2, 2)), dma, dma,
@@ -590,13 +676,19 @@
             collective_id=0, has_side_effects=True, vmem_limit_bytes=63 * 2**20
         ),
     )(
-        frames[:, 0].transpose(0, 2, 1, 3),
-        weight[0],
-        cotangent[:, 0].transpose(0, 2, 1, 3),
+        frames.reshape(STEPS, PIX, C),
+        weight.reshape(9, 2, C, GC),
+        cotangent.reshape(STEPS, PIX, C),
     )
-    hidden = hidden.transpose(0, 2, 1, 3)
-    grads = grads.transpose(0, 2, 1, 3)
-    return hidden[None, :, None], grads[None, :, None], weight_grad[None]
+    hidden, grads, weight_grad = pl.pallas_call(
+        copy_out,
+        out_shape=(maps, maps, jax.ShapeDtypeStruct((HALF, GC), F32)),
+        in_specs=[pl.BlockSpec(memory_space=pl.ANY)] * 3,
+        out_specs=(pl.BlockSpec(memory_space=pl.ANY),) * 3,
+        scratch_shapes=[dma((3,))],
+    )(hidden, grads, weight_grad)
+    tiled = (1, STEPS, 1, ROWS, COLS, C)
+    return hidden.reshape(tiled), grads.reshape(tiled), weight_grad[None]
 
 
 def solution(mesh):

time: 160 us -> 183 us (1.14)
  Pallas kernels: 152 us -> 182 us
  local copies, waits for them, and re-layouts: 7.83 us -> 0 us
    pallas_call x0 -> x1, Pallas kernels: none -> 42.8 us  [local(): pl.pallas_call(copy_out, out_shape=(maps, maps, jax.ShapeDtypeStruct((HAL...]
    pallas_call x1, Pallas kernels: 152 us -> 139 us  [local(): pl.pallas_call(kernel, out_shape=(maps, maps, jax.ShapeDtypeStruct((HALF,...]
    unnamed x3 -> x0, local copies, waits for them, and re-layouts: 5.66 us -> none
    transpose x1 -> x0, local copies, waits for them, and re-layouts: 2.16 us -> none  [local(): cotangent[:, 0].transpose(0, 2, 1, 3)]
where the time goes in v2:
time: 183 us
  Pallas kernels  182 us (99%)
    pallas_call x1, Pallas kernels, local(): pl.pallas_call(kernel, out_shape=(maps, maps, jax.ShapeDtypeStruct((HALF,...  139 us
    pallas_call x1, Pallas kernels, local(): pl.pallas_call(copy_out, out_shape=(maps, maps, jax.ShapeDtypeStruct((HAL...  42.8 us

profile of v2, /device:TPU:1, one launch (start us, length us, event | category | flops | bytes accessed | tf_op | source)
XLA Modules:
  0.0 182.7 jit_solution(9161678605526047001)
XLA Ops:
  0.6 139.3 %shard_map.58 = (bf16[6,128,256]{2,1,0:T(8,128)(2,1)}, bf16[6,128,256]{2,1,0:T(8,128)(2,1)}, f32[144,1024]{1,0:T(8,128)}) custom-call(bf16[6,128,256]{2,1,0:T(8,128)(2,1)} %bitcast.11, bf16[9,2,256,1024]{3,2,1,0:T(8,128)(2,1)} %bitcast.10, bf16[6,128,256]{2,1,0:T(8,128)(2,1)} %bitcast.12), custom_call_target="tpu_custom_call" | custom-call | tf_op jit(solution)/shard_map/pallas_call | solution.py:615
  139.9 42.8 %shard_map.59 = (bf16[6,128,256]{2,1,0:T(8,128)(2,1)}, bf16[6,128,256]{2,1,0:T(8,128)(2,1)}, f32[144,1024]{1,0:T(8,128)}) custom-call(bf16[6,128,256]{2,1,0:T(8,128)(2,1)} %get-tuple-element.9.a, bf16[6,128,256]{2,1,0:T(8,128)(2,1)} %get-tuple-element.10.b, f32[144,1024]{1,0:T(8,128)} %get-tuple-element.11.c), custom_call_target="tpu_custom_call" | custom-call | tf_op jit(solution)/shard_map/pallas_call | solution.py:683

commit v3 on v2

--- a/solution.py
+++ b/solution.py
@@ -598,11 +598,16 @@
     gin_copy.wait()
 
 
-def copy_out(a, b, c, a_out, b_out, c_out, sem):
-    copies = [pltpu.make_async_copy(*pair, sem.at[n]) for n, pair in enumerate(((a, a_out), (b, b_out), (c, c_out)))]
-    for copy in copies:
+def copy_out(a, b, c, a_out, b_out, c_out, a_held, b_held, c_held, in_sem, out_sem):
+    ways = ((a, a_held, a_out), (b, b_held, b_out), (c, c_held, c_out))
+    come = [pltpu.make_async_copy(way[0], way[1], in_sem.at[n]) for n, way in enumerate(ways)]
+    leave = [pltpu.make_async_copy(way[1], way[2], out_sem.at[n]) for n, way in enumerate(ways)]
+    for copy in come:
         copy.start()
-    for copy in copies:
+    for arrived, copy in zip(come, leave):
+        arrived.wait()
+        copy.start()
+    for copy in leave:
         copy.wait()
 
 
@@ -685,7 +690,7 @@
         out_shape=(maps, maps, jax.ShapeDtypeStruct((HALF, GC), F32)),
         in_specs=[pl.BlockSpec(memory_space=pl.ANY)] * 3,
         out_specs=(pl.BlockSpec(memory_space=pl.ANY),) * 3,
-        scratch_shapes=[dma((3,))],
+        scratch_shapes=[vmem((STEPS, PIX, C), BF16), vmem((STEPS, PIX, C), BF16), vmem((HALF, GC), F32), dma((3,)), dma((3,))],
     )(hidden, grads, weight_grad)
     tiled = (1, STEPS, 1, ROWS, COLS, C)
     return hidden.reshape(tiled), grads.reshape(tiled), weight_grad[None]

time: 183 us -> 142 us (0.78)
  Pallas kernels: 182 us -> 141 us
    pallas_call x1, Pallas kernels: 42.8 us -> 2.17 us  [local(): pl.pallas_call(copy_out, out_shape=(maps, maps, jax.ShapeDtypeStruct((HAL...]
where the time goes in v3:
time: 142 us
  Pallas kernels  141 us (99%)
    pallas_call x1, Pallas kernels, local(): pl.pallas_call(kernel, out_shape=(maps, maps, jax.ShapeDtypeStruct((HALF,...  139 us

profile of v3, /device:TPU:1, one launch (start us, length us, event | category | flops | bytes accessed | tf_op | source)
XLA Modules:
  0.0 142.1 jit_solution(10522384271420962593)
XLA Ops:
  0.6 139.3 %shard_map.58 = (bf16[6,128,256]{2,1,0:T(8,128)(2,1)}, bf16[6,128,256]{2,1,0:T(8,128)(2,1)}, f32[144,1024]{1,0:T(8,128)}) custom-call(bf16[6,128,256]{2,1,0:T(8,128)(2,1)} %bitcast.11, bf16[9,2,256,1024]{3,2,1,0:T(8,128)(2,1)} %bitcast.10, bf16[6,128,256]{2,1,0:T(8,128)(2,1)} %bitcast.12), custom_call_target="tpu_custom_call" | custom-call | tf_op jit(solution)/shard_map/pallas_call | solution.py:620
  139.9 2.2 %shard_map.59 = (bf16[6,128,256]{2,1,0:T(8,128)(2,1)}, bf16[6,128,256]{2,1,0:T(8,128)(2,1)}, f32[144,1024]{1,0:T(8,128)}) custom-call(bf16[6,128,256]{2,1,0:T(8,128)(2,1)} %get-tuple-element.9.a, bf16[6,128,256]{2,1,0:T(8,128)(2,1)} %get-tuple-element.10.b, f32[144,1024]{1,0:T(8,128)} %get-tuple-element.11.c), custom_call_target="tpu_custom_call" | custom-call | tf_op jit(solution)/shard_map/pallas_call | solution.py:688

commit v4 on v3

--- a/solution.py
+++ b/solution.py
@@ -18,6 +18,7 @@
 ROWS_OUT = 288
 HALF = 144
 FORGET_SHIFT = 1.0
+PIECE = ((2, 0), (1, 0), (2, 1), (0, 0), (0, 1), (2, 2), (1, 1), (2, 3))
 DIRS = ((-1, -1), (-1, 0), (-1, 1), (0, -1), (0, 1), (1, -1), (1, 0), (1, 1))
 
 
@@ -27,13 +28,17 @@
 
 def kernel(
     frames, weight, cotangent, hid_out, gin_out, wg_out,
-    w, wt, acc, xc, xst, xrim, hs, hst, hrim, st, pst, act, cell, squash, up, gates, pg, hrow, gin,
-    rrim, urim, grim, rstage, gstage, gown, gsum, spread,
+    w, wt, acc, xc, x_rows, x_corners, xrim0, xrim1, xrim2, hs, h_rows, h_corners, hrim0, hrim1, hrim2, st, pst, act, cell, squash, up, gates, pg, hrow, gin,
+    rrim0, rrim1, rrim2, urim0, urim1, urim2, grim0, grim1, grim2,
+    rstage0, rstage1, rstage2, gstage0, gstage1, gstage2, gown, gsum, spread,
     recurrent, carried, sums, part, from_l, from_r, full_l, full_r, total, from2_l, from2_r, full2_l, full2_r, res, pres,
     w_sem, in_sem, out_sem, xs_send, fr_send, hs_send, rs_send, us_send, gs_send, ps_send, pg_send,
     xc_recv, x_recv, h_recv, r_recv_rim, u_recv_rim, g_recv_rim, u_recv, ps_recv, pg_recv,
     t_send, t_recv, f_send, f_recv, t2_send, t2_recv, f2_send, f2_recv, r_send, r_recv,
 ):
+    xrim, hrim, rrim = (xrim0, xrim1, xrim2), (hrim0, hrim1, hrim2), (rrim0, rrim1, rrim2)
+    urim, grim = (urim0, urim1, urim2), (grim0, grim1, grim2)
+    rstage, gstage = (rstage0, rstage1, rstage2), (gstage0, gstage1, gstage2)
     layer = lax.axis_index("layer")
     tile = lax.axis_index("tile")
     trow, tcol = tile // 8, lax.rem(tile, 8)
@@ -107,11 +112,9 @@
 
         @pl.when(jnp.logical_not(found))
         def _(d=d):
-            xrim[d] = jnp.zeros((STEPS, ROWS, C), BF16)
-            hrim[d] = jnp.zeros((STEPS, ROWS, C), BF16)
-            rrim[d] = jnp.zeros((STEPS, ROWS, C), F32)
-            urim[d] = jnp.zeros((STEPS, ROWS, C), F32)
-            grim[d] = jnp.zeros((STEPS, ROWS, C), F32)
+            kind, n = PIECE[d]
+            for rims in (xrim, hrim, rrim, urim, grim):
+                rims[kind][n] = jnp.zeros(rims[kind].shape[1:], rims[kind].dtype)
 
     pl.semaphore_wait(barrier, expected)
 
@@ -124,33 +127,46 @@
         dst[1, 1:9] = value.astype(BF16).reshape(COLS, ROWS, C)
         dst[2, 1:9] = pltpu.roll(value, PIX - 1, 0).astype(BF16).reshape(COLS, ROWS, C)
 
-    def put_rim(dst, rim, t):
-        top = rim[1, t].astype(F32)[0:8].reshape(COLS, 1, C)
-        bottom = rim[6, t].astype(F32)[0:8].reshape(COLS, 1, C)
+    def row_of(rims, n, t):
+        held = rims[1][n, t].astype(F32)
+        if held.shape[1] == C:
+            return held
+        return jnp.concatenate([held[0:8], held[8:16]], axis=1)
+
+    def corner_of(rims, n, t):
+        held = rims[2][n, t]
+        return jnp.concatenate([held[0:1], held[1:2]], axis=1)
+
+    def fold_row(row):
+        return jnp.concatenate([row[:, 0:128], row[:, 128:256]], axis=0)
+
+    def put_rim(dst, rims, t):
+        top = row_of(rims, 0, t).reshape(COLS, 1, C)
+        bottom = row_of(rims, 1, t).reshape(COLS, 1, C)
         dst[0, 1:9] = jnp.where(is_top[None], top, dst[0, 1:9].astype(F32)).astype(BF16)
         dst[2, 1:9] = jnp.where(is_bottom[None], bottom, dst[2, 1:9].astype(F32)).astype(BF16)
-        for column, side, above, below, at in ((0, 3, 0, 5, 7), (9, 4, 2, 7, 0)):
-            value = rim[side, t].astype(F32)
-            upper = rim[above, t].astype(F32)[at : at + 1]
-            lower = rim[below, t].astype(F32)[at : at + 1]
-            dst[0, column] = jnp.where(is_top, upper, pltpu.roll(value, 1, 0)).astype(BF16)
-            dst[1, column] = rim[side, t]
+        for n, column in ((0, 0), (1, 9)):
+            value = rims[0][n, t].astype(F32)
+            dst[0, column] = jnp.where(is_top, corner_of(rims, n, t), pltpu.roll(value, 1, 0)).astype(BF16)
+            dst[1, column] = rims[0][n, t]
+            lower = corner_of(rims, n + 2, t)
             dst[2, column] = jnp.where(is_bottom, lower, pltpu.roll(value, ROWS - 1, 0)).astype(BF16)
 
-    def put_stage(stage, t, value):
+    def put_stage(rows, corners, t, value):
         cut = value.reshape(COLS, ROWS, C)
-        for side, at in ((0, 0), (1, ROWS - 1)):
-            row = cut[:, at, :]
-            stage[t, side] = jnp.concatenate([row, row], axis=0).astype(BF16)
-
-    def add_rims(value, rim, t):
+        rows[0, t] = fold_row(cut[:, 0, :]).astype(BF16)
+        rows[1, t] = fold_row(cut[:, ROWS - 1, :]).astype(BF16)
+        for n, at in enumerate((0, PIX - ROWS, ROWS - 1, PIX - 1)):
+            corners[n, t] = fold_row(value[at : at + 1])
+
+    def add_rims(value, rims, t):
         cut = value.reshape(COLS, ROWS, C)
-        cut = cut + jnp.where(is_top[None], rim[1, t, 0:8].reshape(COLS, 1, C), 0.0)
-        cut = cut + jnp.where(is_bottom[None], rim[6, t, 0:8].reshape(COLS, 1, C), 0.0)
+        cut = cut + jnp.where(is_top[None], row_of(rims, 0, t).reshape(COLS, 1, C), 0.0)
+        cut = cut + jnp.where(is_bottom[None], row_of(rims, 1, t).reshape(COLS, 1, C), 0.0)
         sides = []
-        for side, above, below in ((3, 0, 5), (4, 2, 7)):
-            column = rim[side, t] + jnp.where(is_top, rim[above, t, 0:1], 0.0)
-            sides.append((column + jnp.where(is_bottom, rim[below, t, 0:1], 0.0))[None])
+        for n in range(2):
+            column = rims[0][n, t].astype(F32) + jnp.where(is_top, corner_of(rims, n, t), 0.0)
+            sides.append((column + jnp.where(is_bottom, corner_of(rims, n + 2, t), 0.0))[None])
         cut = jnp.concatenate([cut[0:1] + sides[0], cut[1:7], cut[7:8] + sides[1]], axis=0)
         return cut.reshape(PIX, C)
 
@@ -160,47 +176,51 @@
     def by_rows(value):
         return jnp.transpose(value.reshape(COLS, ROWS, C), (1, 0, 2)).reshape(PIX, C).astype(BF16)
 
-    def rim_source(d, store, stage, t):
-        dy, dx = DIRS[d]
-        if dy < 0:
-            return stage.at[t, 0]
-        if dy > 0:
-            return stage.at[t, 1]
-        return store.at[t, 0 if dx < 0 else COLS - 1]
-
-    def send_rims(store, stage, rim, t, send, recv, to_layer, first):
+    def map_rims(store, rows, corners, t):
+        return (store.at[t, 0], store.at[t, COLS - 1]), (rows.at[0, t], rows.at[1, t]), [corners.at[n, t] for n in range(4)]
+
+    def grad_rims(stage):
+        return [[held.at[n] for n in range(held.shape[0])] for held in stage]
+
+    def rim_copies(source, rims, t, send, recv, to_layer, act_on):
         for d in range(8):
             found, other = there(d)
+            kind, n = PIECE[d]
+            far = PIECE[7 - d][1]
 
             @pl.when(found)
-            def _(d=d, other=other):
-                copy = remote(
-                    rim_source(d, store, stage, t), rim.at[7 - d, t], send.at[d], recv.at[7 - d, t], to_layer, other
-                )
-
-                @pl.when(jnp.logical_not(first))
-                def _():
-                    copy.wait_send()
-
-                copy.start()
-
-    def end_rims(store, stage, rim, send, recv):
+            def _(d=d, other=other, kind=kind, n=n, far=far):
+                act_on(remote(
+                    source[kind][n], rims[kind].at[far, t], send.at[d], recv.at[7 - d, t], to_layer, other
+                ))
+
+    def rim_arrivals(rims, t, send, recv):
         for d in range(8):
             found, other = there(d)
+            kind, n = PIECE[d]
 
             @pl.when(found)
-            def _(d=d, other=other):
-                remote(
-                    rim_source(d, store, stage, 0), rim.at[7 - d, 0], send.at[d], recv.at[7 - d, 0], layer, other
-                ).wait_send()
-
-    def wait_rims(rim, t, send, recv):
-        for d in range(8):
-            found, other = there(d)
-
-            @pl.when(found)
-            def _(d=d, other=other):
-                remote(rim.at[d, t], rim.at[d, t], send.at[d], recv.at[d, t], layer, other).wait_recv()
+            def _(d=d, other=other, kind=kind, n=n):
+                here = rims[kind].at[n, t]
+                remote(here, here, send.at[d], recv.at[d, t], layer, other).wait_recv()
+
+    def begin(copy):
+        copy.start()
+
+    def settle(copy):
+        copy.wait_send()
+
+    def send_map(store, rows, corners, rims, t, send, recv, to_layer):
+        source = map_rims(store, rows, corners, t)
+
+        @pl.when(t > 0)
+        def _():
+            rim_copies(source, rims, t, send, recv, to_layer, settle)
+
+        rim_copies(source, rims, t, send, recv, to_layer, begin)
+
+    def end_map(store, rows, corners, rims, send, recv, to_layer):
+        rim_copies(map_rims(store, rows, corners, 0), rims, 0, send, recv, to_layer, settle)
 
     def turn_weight():
         def one(k, _):
@@ -217,12 +237,12 @@
         def one(t, _):
             value = by_columns(gin[t])
             xc[t] = value.astype(BF16)
-            put_stage(xst, t, value.reshape(PIX, C))
-            send_rims(xc, xst, xrim, t, fr_send, x_recv, layer, t == 0)
+            put_stage(x_rows, x_corners, t, value.reshape(PIX, C))
+            send_map(xc, x_rows, x_corners, xrim, t, fr_send, x_recv, layer)
             return 0
 
         lax.fori_loop(0, STEPS, one, 0)
-        end_rims(xc, xst, xrim, fr_send, x_recv)
+        end_map(xc, x_rows, x_corners, xrim, fr_send, x_recv, layer)
 
     for copy in w_copies:
         copy.wait()
@@ -254,13 +274,13 @@
             remote(xc.at[t], xc.at[t], xs_send.at[8], xc_recv.at[t], layer - 1, tile).wait_recv()
 
         put_centre(st.at[t, 0], xc[t].astype(F32).reshape(PIX, C))
-        wait_rims(xrim, t, xs_send, x_recv)
+        rim_arrivals(xrim, t, xs_send, x_recv)
         put_rim(st.at[t, 0], xrim, t)
         sums[...] = jnp.dot(patches(t, 0), w[0].reshape(9 * C, GC), preferred_element_type=F32)
 
         @pl.when(t > 0)
         def _():
-            wait_rims(hrim, t - 1, hs_send, h_recv)
+            rim_arrivals(hrim, t - 1, hs_send, h_recv)
             put_rim(st.at[t, 1], hrim, t - 1)
             mate_patches(t - 1).wait_send()
             sums[...] += jnp.dot(patches(t, 1), w[1].reshape(9 * C, GC), preferred_element_type=F32)
@@ -273,11 +293,11 @@
         squashed = jnp.tanh(fresh)
         hidden = out_gate * squashed
         hs[t] = hidden.astype(BF16).reshape(COLS, ROWS, C)
-        put_stage(hst, t, hidden)
+        put_stage(h_rows, h_corners, t, hidden)
 
         @pl.when(t < STEPS - 1)
         def _():
-            send_rims(hs, hst, hrim, t, hs_send, h_recv, layer, t == 0)
+            send_map(hs, h_rows, h_corners, hrim, t, hs_send, h_recv, layer)
 
         @pl.when(layer < 3)
         def _():
@@ -286,7 +306,7 @@
                 above_map(t - 1).wait_send()
 
             above_map(t).start()
-            send_rims(hs, hst, xrim, t, xs_send, x_recv, layer + 1, t == 0)
+            send_map(hs, h_rows, h_corners, xrim, t, xs_send, x_recv, layer + 1)
 
         mate_patches(t).start()
         act[t, :, 0:C] = in_gate
@@ -305,7 +325,7 @@
 
     lax.fori_loop(0, STEPS, forward, 0)
     mate_patches(STEPS - 1).wait_send()
-    end_rims(hs, hst, hrim, hs_send, h_recv)
+    end_map(hs, h_rows, h_corners, hrim, hs_send, h_recv, layer)
 
     hid_copy = pltpu.make_async_copy(hrow, hid_out, out_sem.at[0])
     hid_copy.start()
@@ -314,7 +334,7 @@
     def _():
         turn_weight()
         above_map(STEPS - 1).wait_send()
-        end_rims(hs, hst, xrim, xs_send, x_recv)
+        end_map(hs, h_rows, h_corners, xrim, xs_send, x_recv, layer + 1)
 
     mine = pl.ds(pl.multiple_of(core * 512, 512), 512)
     theirs = pl.ds(pl.multiple_of((1 - core) * 512, 512), 512)
@@ -349,48 +369,23 @@
         upper, lower = spread[0], spread[2]
         centre = spread[1] + jnp.where(row == ROWS - 1, 0.0, pltpu.roll(upper, PIX + 2 * ROWS - 1, 0))
         centre = centre + jnp.where(row == 0, 0.0, pltpu.roll(lower, 1, 0))
-        stage[1, 0:8] = upper.reshape(COLS + 2, ROWS, C)[1:9, 0, :]
-        stage[6, 0:8] = lower.reshape(COLS + 2, ROWS, C)[1:9, ROWS - 1, :]
-        stage[3] = centre[0:ROWS]
-        stage[4] = centre[PIX + ROWS :]
-        for d, source, at in ((0, upper, 0), (2, upper, PIX + ROWS), (5, lower, ROWS - 1), (7, lower, PIX + 2 * ROWS - 1)):
-            stage[d, 0:8] = jnp.broadcast_to(source[at : at + 1], (8, C))
+        rows = (upper.reshape(COLS + 2, ROWS, C)[1:9, 0, :], lower.reshape(COLS + 2, ROWS, C)[1:9, ROWS - 1, :])
+        stage[0][0] = centre[0:ROWS].astype(stage[0].dtype)
+        stage[0][1] = centre[PIX + ROWS :].astype(stage[0].dtype)
+        for m in range(2):
+            stage[1][m] = (rows[m] if stage[1].shape[2] == C else fold_row(rows[m])).astype(stage[1].dtype)
+        ends = ((upper, 0), (upper, PIX + ROWS), (lower, ROWS - 1), (lower, PIX + 2 * ROWS - 1))
+        for m, (source, at) in enumerate(ends):
+            stage[2][m] = fold_row(source[at : at + 1])
         return centre[ROWS : PIX + ROWS]
 
-    def rim_copies(stage, rim, t, send, recv, to_layer, act_on):
-        for d in range(8):
-            found, other = there(d)
-            rows = pl.ds(0, ROWS if d in (3, 4) else 8)
-
-            @pl.when(found)
-            def _(d=d, other=other, rows=rows):
-                act_on(remote(
-                    stage.at[d, rows], rim.at[7 - d, t, rows], send.at[d], recv.at[7 - d, t], to_layer, other
-                ))
-
-    def rim_arrivals(rim, t, send, recv):
-        for d in range(8):
-            found, other = there(d)
-            rows = pl.ds(0, ROWS if d in (3, 4) else 8)
-
-            @pl.when(found)
-            def _(d=d, other=other, rows=rows):
-                here = rim.at[d, t, rows]
-                remote(here, here, send.at[d], recv.at[d, t], layer, other).wait_recv()
-
-    def begin(copy):
-        copy.start()
-
-    def settle(copy):
-        copy.wait_send()
-
     def settle_inputs(t):
-        rim_copies(gstage, grim, t, gs_send, g_recv_rim, layer, settle)
+        rim_copies(grad_rims(gstage), grim, t, gs_send, g_recv_rim, layer, settle)
 
         @pl.when(layer > 0)
         def _():
             below_grad(t).wait_send()
-            rim_copies(gstage, urim, t, us_send, u_recv_rim, layer - 1, settle)
+            rim_copies(grad_rims(gstage), urim, t, us_send, u_recv_rim, layer - 1, settle)
 
     def finish_inputs(t):
         rim_arrivals(grim, t, gs_send, g_recv_rim)
@@ -398,7 +393,8 @@
 
     @pl.when(layer == 3)
     def _():
-        urim[...] = jnp.zeros_like(urim)
+        for held in urim:
+            held[...] = jnp.zeros_like(held)
 
     def backward(i, _):
         t = STEPS - 1 - i
@@ -436,10 +432,10 @@
         def _():
             @pl.when(i > 0)
             def _():
-                rim_copies(rstage, rrim, t + 1, rs_send, r_recv_rim, layer, settle)
+                rim_copies(grad_rims(rstage), rrim, t + 1, rs_send, r_recv_rim, layer, settle)
 
             recurrent[...] = spread_out(t, 1, rstage)
-            rim_copies(rstage, rrim, t, rs_send, r_recv_rim, layer, begin)
+            rim_copies(grad_rims(rstage), rrim, t, rs_send, r_recv_rim, layer, begin)
 
         @pl.when(i > 0)
         def _():
@@ -451,9 +447,9 @@
         @pl.when(layer > 0)
         def _():
             below_grad(t).start()
-            rim_copies(gstage, urim, t, us_send, u_recv_rim, layer - 1, begin)
-
-        rim_copies(gstage, grim, t, gs_send, g_recv_rim, layer, begin)
+            rim_copies(grad_rims(gstage), urim, t, us_send, u_recv_rim, layer - 1, begin)
+
+        rim_copies(grad_rims(gstage), grim, t, gs_send, g_recv_rim, layer, begin)
         gsum[t] = own
 
         @pl.when(i > 0)
@@ -469,7 +465,7 @@
         return 0
 
     lax.fori_loop(0, STEPS, backward, 0)
-    rim_copies(rstage, rrim, 1, rs_send, r_recv_rim, layer, settle)
+    rim_copies(grad_rims(rstage), rrim, 1, rs_send, r_recv_rim, layer, settle)
     wait_mate(0)
     mate_gates(0).wait_send()
     for p in range(3):
@@ -617,6 +613,14 @@
     dma = pltpu.SemaphoreType.DMA
     shape = (STEPS, COLS, ROWS, C)
     block = (ROWS_OUT, 256)
+
+    def rims_of(dtype):
+        row = (ROWS, 128) if dtype == BF16 else (8, C)
+        return vmem((2, STEPS, ROWS, C), dtype), vmem((2, STEPS) + row, dtype), vmem((4, STEPS, 2, 128), F32)
+
+    def stage_of(steps):
+        return vmem((2, steps, ROWS, 128), BF16), vmem((4, steps, 2, 128), F32)
+
     hidden, grads, weight_grad = pl.pallas_call(
         kernel,
         out_shape=(maps, maps, jax.ShapeDtypeStruct((HALF, GC), F32)),
@@ -631,11 +635,11 @@
             vmem((2, 9, GC, C), BF16),
             vmem((4608, 512), F32),
             vmem(shape, BF16),
-            vmem((STEPS, 2, ROWS, C), BF16),
-            vmem((8, STEPS, ROWS, C), BF16),
+            *stage_of(STEPS),
+            *rims_of(BF16),
             vmem(shape, BF16),
-            vmem((STEPS, 2, ROWS, C), BF16),
-            vmem((8, STEPS, ROWS, C), BF16),
+            *stage_of(STEPS),
+            *rims_of(BF16),
             vmem((STEPS, 2, 3, COLS + 2, ROWS, C), BF16),
             vmem((STEPS, 2, 3, COLS + 2, ROWS, C), BF16),
             vmem((STEPS, PIX, GC), F32),
@@ -646,11 +650,11 @@
             vmem((STEPS, PIX, 512), BF16),
             vmem((STEPS, PIX, C), BF16),
             vmem((STEPS, PIX, C), BF16),
-            vmem((8, STEPS, ROWS, C), F32),
-            vmem((8, STEPS, ROWS, C), F32),
-            vmem((8, STEPS, ROWS, C), F32),
-            vmem((8, ROWS, C), F32),
-            vmem((8, ROWS, C), F32),
+            *rims_of(F32),
+            *rims_of(BF16),
+            *rims_of(BF16),
+            vmem((2, ROWS, C), F32), vmem((2, 8, C), F32), vmem((4, 2, 128), F32),
+            vmem((2, ROWS, C), BF16), vmem((2, ROWS, 128), BF16), vmem((4, 2, 128), F32),
             vmem(shape, BF16),
             vmem((STEPS, PIX, C), F32),
             vmem((3, PIX + 2 * ROWS, C), F32),

time: 142 us -> 135 us (0.951)
  Pallas kernels: 141 us -> 135 us
    pallas_call x1, Pallas kernels: 139 us -> 132 us  [local(): pl.pallas_call(kernel, out_shape=(maps, maps, jax.ShapeDtypeStruct((HALF,...]
where the time goes in v4:
time: 135 us
  Pallas kernels  135 us (100%)
    pallas_call x1, Pallas kernels, local(): pl.pallas_call(kernel, out_shape=(maps, maps, jax.ShapeDtypeStruct((HALF,...  132 us

profile of v4, /device:TPU:1, one launch (start us, length us, event | category | flops | bytes accessed | tf_op | source)
XLA Modules:
  0.0 135.3 jit_solution(17918894088539002763)
XLA Ops:
  0.6 132.5 %shard_map.58 = (bf16[6,128,256]{2,1,0:T(8,128)(2,1)}, bf16[6,128,256]{2,1,0:T(8,128)(2,1)}, f32[144,1024]{1,0:T(8,128)}) custom-call(bf16[6,128,256]{2,1,0:T(8,128)(2,1)} %bitcast.11, bf16[9,2,256,1024]{3,2,1,0:T(8,128)(2,1)} %bitcast.10, bf16[6,128,256]{2,1,0:T(8,128)(2,1)} %bitcast.12), custom_call_target="tpu_custom_call" | custom-call | tf_op jit(solution)/shard_map/pallas_call | solution.py:624
  133.1 2.2 %shard_map.59 = (bf16[6,128,256]{2,1,0:T(8,128)(2,1)}, bf16[6,128,256]{2,1,0:T(8,128)(2,1)}, f32[144,1024]{1,0:T(8,128)}) custom-call(bf16[6,128,256]{2,1,0:T(8,128)(2,1)} %get-tuple-element.9.a, bf16[6,128,256]{2,1,0:T(8,128)(2,1)} %get-tuple-element.10.b, f32[144,1024]{1,0:T(8,128)} %get-tuple-element.11.c), custom_call_target="tpu_custom_call" | custom-call | tf_op jit(solution)/shard_map/pallas_call | solution.py:692

commit v5 on v4

--- a/solution.py
+++ b/solution.py
@@ -31,10 +31,10 @@
     w, wt, acc, xc, x_rows, x_corners, xrim0, xrim1, xrim2, hs, h_rows, h_corners, hrim0, hrim1, hrim2, st, pst, act, cell, squash, up, gates, pg, hrow, gin,
     rrim0, rrim1, rrim2, urim0, urim1, urim2, grim0, grim1, grim2,
     rstage0, rstage1, rstage2, gstage0, gstage1, gstage2, gown, gsum, spread,
-    recurrent, carried, sums, part, from_l, from_r, full_l, full_r, total, from2_l, from2_r, full2_l, full2_r, res, pres,
+    recurrent, carried, sums, part, from_l, from_r, full_l, full_r, total, got,
     w_sem, in_sem, out_sem, xs_send, fr_send, hs_send, rs_send, us_send, gs_send, ps_send, pg_send,
     xc_recv, x_recv, h_recv, r_recv_rim, u_recv_rim, g_recv_rim, u_recv, ps_recv, pg_recv,
-    t_send, t_recv, f_send, f_recv, t2_send, t2_recv, f2_send, f2_recv, r_send, r_recv,
+    t_send, t_recv, f_send, f_recv, d_send, d_recv,
 ):
     xrim, hrim, rrim = (xrim0, xrim1, xrim2), (hrim0, hrim1, hrim2), (rrim0, rrim1, rrim2)
     urim, grim = (urim0, urim1, urim2), (grim0, grim1, grim2)
@@ -64,10 +64,10 @@
             device_id={"layer": to_layer, "tile": to_tile}, device_id_type=MESH,
         )
 
-    def at_ring(along_y, step):
+    def at_ring(along_y, step, which):
         if along_y:
-            return trow * 8 + lax.rem(ypos + step, 4) * 2 + core
-        return lax.rem(trow + step, 4) * 8 + tcol
+            return trow * 8 + lax.rem(ypos + step, 4) * 2 + which
+        return lax.rem(trow + step, 4) * 8 + ypos * 2 + which
 
     @pl.when(layer == 0)
     def _():
@@ -99,8 +99,9 @@
     expected += greet(layer > 0, layer - 1, tile)
     expected += greet(layer < 3, layer + 1, tile)
     for along_y in (True, False):
-        for step in (1, 3):
-            expected += greet(jnp.bool_(True), layer, at_ring(along_y, step))
+        for step in (1, 2, 3):
+            for other in range(2):
+                expected += greet(jnp.bool_(True), layer, at_ring(along_y, step, other))
 
     acc[...] = jnp.zeros_like(acc)
     recurrent[...] = jnp.zeros_like(recurrent)
@@ -238,11 +239,10 @@
             value = by_columns(gin[t])
             xc[t] = value.astype(BF16)
             put_stage(x_rows, x_corners, t, value.reshape(PIX, C))
-            send_map(xc, x_rows, x_corners, xrim, t, fr_send, x_recv, layer)
+            rim_copies(map_rims(xc, x_rows, x_corners, t), xrim, t, fr_send.at[t], x_recv, layer, begin)
             return 0
 
         lax.fori_loop(0, STEPS, one, 0)
-        end_map(xc, x_rows, x_corners, xrim, fr_send, x_recv, layer)
 
     for copy in w_copies:
         copy.wait()
@@ -335,6 +335,14 @@
         turn_weight()
         above_map(STEPS - 1).wait_send()
         end_map(hs, h_rows, h_corners, xrim, xs_send, x_recv, layer + 1)
+
+    @pl.when(layer == 0)
+    def _():
+        def one(t, _):
+            rim_copies(map_rims(xc, x_rows, x_corners, t), xrim, t, fr_send.at[t], x_recv, layer, settle)
+            return 0
+
+        lax.fori_loop(0, STEPS, one, 0)
 
     mine = pl.ds(pl.multiple_of(core * 512, 512), 512)
     theirs = pl.ds(pl.multiple_of((1 - core) * 512, 512), 512)
@@ -391,6 +399,22 @@
         rim_arrivals(grim, t, gs_send, g_recv_rim)
         gin[t] = by_rows(add_rims(gsum[t], grim, t))
 
+    def input_part(t):
+        @pl.when(t < STEPS - 1)
+        def _():
+            settle_inputs(t + 1)
+
+        own = spread_out(t, 0, gstage)
+        gown[t] = own.astype(BF16).reshape(COLS, ROWS, C)
+
+        @pl.when(layer > 0)
+        def _():
+            below_grad(t).start()
+            rim_copies(grad_rims(gstage), urim, t, us_send, u_recv_rim, layer - 1, begin)
+
+        rim_copies(grad_rims(gstage), grim, t, gs_send, g_recv_rim, layer, begin)
+        gsum[t] = own
+
     @pl.when(layer == 3)
     def _():
         for held in urim:
@@ -437,51 +461,26 @@
             recurrent[...] = spread_out(t, 1, rstage)
             rim_copies(grad_rims(rstage), rrim, t, rs_send, r_recv_rim, layer, begin)
 
-        @pl.when(i > 0)
-        def _():
-            settle_inputs(t + 1)
-
-        own = spread_out(t, 0, gstage)
-        gown[t] = own.astype(BF16).reshape(COLS, ROWS, C)
-
-        @pl.when(layer > 0)
-        def _():
-            below_grad(t).start()
-            rim_copies(grad_rims(gstage), urim, t, us_send, u_recv_rim, layer - 1, begin)
-
-        rim_copies(grad_rims(gstage), grim, t, gs_send, g_recv_rim, layer, begin)
-        gsum[t] = own
-
-        @pl.when(i > 0)
-        def _():
-            wait_mate(t + 1)
+        @pl.when((layer > 0) | (t > 0))
+        def _():
+            input_part(t)
+
+        @pl.when(t > 0)
+        def _():
+            wait_mate(t)
             for p in range(3):
                 for q in range(3):
                     for n in range(2):
                         low = 512 * (3 * p + q) + C * n
-                        acc[low : low + C] += weight_terms(t + 1, n, p, q)
+                        acc[low : low + C] += weight_terms(t, n, p, q)
+
+        @pl.when((i > 0) & (t > 0))
+        def _():
             finish_inputs(t + 1)
 
         return 0
 
     lax.fori_loop(0, STEPS, backward, 0)
-    rim_copies(grad_rims(rstage), rrim, 1, rs_send, r_recv_rim, layer, settle)
-    wait_mate(0)
-    mate_gates(0).wait_send()
-    for p in range(3):
-        for q in range(3):
-            for n in range(2):
-                start = 512 * (3 * p + q) + C * n
-                value = (acc[start : start + C] + weight_terms(0, n, p, q)).astype(BF16)
-                low = start
-                while low < start + C:
-                    block = low // ROWS_OUT
-                    high = min(start + C, ROWS_OUT * (block + 1))
-                    rows = slice(low - ROWS_OUT * block, high - ROWS_OUT * block)
-                    z, y = block // 4, block % 4
-                    part[0, y, z, rows] = value[low - start : high - start, 0:256]
-                    part[1, z, y, rows] = value[low - start : high - start, 256:512]
-                    low = high
 
     def plus(left, right):
         return (left.astype(F32) + right.astype(F32)).astype(BF16)
@@ -497,36 +496,63 @@
         sent.append(copy)
         return copy
 
-    def hop(n, first, to_right):
-        return at_ring((n == 0) == first, 1 if to_right else 3)
-
     hand = {}
     full = {}
+
+    def last_terms(half):
+        columns = slice(256 * half, 256 * half + 256)
+        rhs = jnp.concatenate(
+            [gates[0, :, pl.ds(pl.multiple_of(core * 512 + 256 * half, 256), 256)], pg[0, :, columns]], axis=0
+        )
+        for p in range(3):
+            for q in range(3):
+                for n in range(2):
+                    start = 512 * (3 * p + q) + C * n
+                    lhs = jnp.concatenate(
+                        [st[0, n, p, q : q + 8].reshape(PIX, C), pst[0, n, p, q : q + 8].reshape(PIX, C)], axis=0
+                    )
+                    term = lax.dot_general(lhs, rhs, (((0,), (0,)), ((), ())), preferred_element_type=F32)
+                    value = (acc[start : start + C, columns] + term).astype(BF16)
+                    low = start
+                    while low < start + C:
+                        block = low // ROWS_OUT
+                        high = min(start + C, ROWS_OUT * (block + 1))
+                        rows = slice(low - ROWS_OUT * block, high - ROWS_OUT * block)
+                        z, y = block // 4, block % 4
+                        at = (0, y, z, rows) if half == 0 else (1, z, y, rows)
+                        part[at] = value[low - start : high - start]
+                        low = high
+
+    def send_full(n, j, right):
+        a, b = own(n)
+        full[n, j, right] = go(remote(
+            part.at[n, lax.rem(a + (1 if right else 3), 4), lax.rem(b + j, 4)], (full_l if right else full_r).at[n, j],
+            f_send.at[n, j, int(right)], f_recv.at[n, j, int(right)], layer, at_ring(n == 0, 1 if right else 3, core),
+        ))
+
+    wait_mate(0)
+    mate_gates(0).wait_send()
     for n in range(2):
         a, b = own(n)
+        last_terms(n)
         for m in range(2):
             for right in (True, False):
                 j = (rights if right else lefts)[m]
                 hand[n, m, right] = go(remote(
                     part.at[n, lax.rem(a + 2, 4), lax.rem(b + j, 4)], (from_l if right else from_r).at[n, m],
-                    t_send.at[n, m, int(right)], t_recv.at[n, m, int(right)], layer, hop(n, True, right),
+                    t_send.at[n, m, int(right)], t_recv.at[n, m, int(right)], layer,
+                    at_ring(n == 0, 1 if right else 3, core),
                 ))
-
-    def send_full(n, j, right):
-        a, b = own(n)
-        full[n, j, right] = go(remote(
-            part.at[n, lax.rem(a + (1 if right else 3), 4), lax.rem(b + j, 4)], (full_l if right else full_r).at[n, j],
-            f_send.at[n, j, int(right)], f_recv.at[n, j, int(right)], layer, hop(n, True, right),
-        ))
-
-    for m in range(2):
-        for n in range(2):
+        for m in range(2):
             send_full(n, lefts[m], True)
             send_full(n, rights[m], False)
-    finish_inputs(0)
-    gin_copy = pltpu.make_async_copy(gin, gin_out, out_sem.at[1])
-    gin_copy.start()
-    settle_inputs(0)
+
+    @pl.when(layer == 0)
+    def _():
+        input_part(0)
+
+    finish_inputs(1)
+    rim_copies(grad_rims(rstage), rrim, 1, rs_send, r_recv_rim, layer, settle)
     for m in range(2):
         for n in range(2):
             a, b = own(n)
@@ -536,6 +562,10 @@
                 to = (n, lax.rem(a + (1 if right else 3), 4), lax.rem(b + j, 4))
                 part[to] = plus(part[to], (from_l if right else from_r)[n, m])
                 send_full(n, j, right)
+    finish_inputs(0)
+    gin_copy = pltpu.make_async_copy(gin, gin_out, out_sem.at[1])
+    gin_copy.start()
+    settle_inputs(0)
 
     def gather(n, j):
         a, b = own(n)
@@ -545,51 +575,39 @@
             part[n, a, lax.rem(b + j, 4)].astype(F32) + full_l[n, j].astype(F32) + full_r[n, j].astype(F32)
         ).astype(BF16)
 
-    upper, lower = pl.ds(0, HALF), pl.ds(HALF, HALF)
-    hand2 = {}
-    full2 = {}
-
-    def send_full2(n, right, first):
-        rows = lower if right == first else upper
-        full2[n, right, first] = go(remote(
-            total.at[n, 1 if right else 3, rows], (full2_l if right else full2_r).at[n, rows],
-            f2_send.at[n, int(right), int(first)], f2_recv.at[n, int(right), int(first)], layer, hop(n, False, right),
-        ))
-
+    def half_rows(which):
+        return pl.ds(pl.multiple_of(which * HALF, HALF), HALF)
+
+    def to_owner(n, j, which, slot):
+        return remote(
+            total.at[n, j, half_rows(which)], got.at[n, j, core], d_send.at[n, j, slot], d_recv.at[n, j, core],
+            layer, at_ring(n == 1, j, which),
+        )
+
+    for j in (2, 1, 3, 0):
+        for n in range(2):
+            gather(n, j)
+            if j == 0:
+                go(to_owner(n, 0, 1 - core, 0))
+                got[n, 0, core] = total[n, 0, half_rows(core), :]
+            else:
+                for which in range(2):
+                    go(to_owner(n, j, which, which))
     for n in range(2):
-        gather(n, 2)
-        for right in (True, False):
-            hand2[n, right] = go(remote(
-                total.at[n, 2, upper if right else lower], (from2_l if right else from2_r).at[n],
-                t2_send.at[n, int(right)], t2_recv.at[n, int(right)], layer, hop(n, False, right),
-            ))
-    for right in (True, False):
+        remote(got.at[n, 0, 1 - core], got.at[n, 0, 1 - core], d_send.at[n, 0, 0], d_recv.at[n, 0, 1 - core], layer, mate).wait_recv()
+        for j in (1, 3, 2):
+            for which in range(2):
+                here = got.at[n, j, which]
+                remote(here, here, d_send.at[n, j, which], d_recv.at[n, j, which], layer, at_ring(n == 1, 4 - j, which)).wait_recv()
+    for which in range(2):
         for n in range(2):
-            gather(n, 1 if right else 3)
-            send_full2(n, right, True)
-    for n in range(2):
-        for right in (True, False):
-            hand2[n, right].wait_recv()
-            at = (n, 1 if right else 3, upper if right else lower)
-            total[at] = plus(total[at], (from2_l if right else from2_r)[n])
-            send_full2(n, right, False)
-    for n in range(2):
-        gather(n, 0)
-    for n in range(2):
-        for right in (True, False):
-            for first in (True, False):
-                full2[n, right, first].wait_recv()
-        res[:, 256 * n : 256 * n + 256] = plus(
-            total[n, 0].astype(F32) + full2_l[n].astype(F32), full2_r[n]
-        )
-    last = go(remote(
-        res.at[pl.ds(pl.multiple_of((1 - core) * HALF, HALF), HALF)], pres, r_send, r_recv, layer, mate
-    ))
-    wg_out[:, mine] = res[pl.ds(pl.multiple_of(core * HALF, HALF), HALF), :].astype(F32)
-    last.wait_recv()
-    wg_out[:, theirs] = pres[...].astype(F32)
+            low = 512 * which + 256 * n
+            wg_out[:, low : low + 256] = (got[n, 0, which].astype(F32) + got[n, 1, which].astype(F32)) + (
+                got[n, 2, which].astype(F32) + got[n, 3, which].astype(F32)
+            )
     for copy in sent:
         copy.wait_send()
+
     hid_copy.wait()
     gin_copy.wait()
 
@@ -667,19 +685,14 @@
             vmem((2, 4) + block, BF16),
             vmem((2, 4) + block, BF16),
             vmem((2, 4) + block, BF16),
-            vmem((2, HALF, 256), BF16),
-            vmem((2, HALF, 256), BF16),
-            vmem((2,) + block, BF16),
-            vmem((2,) + block, BF16),
-            vmem((ROWS_OUT, 512), BF16),
-            vmem((HALF, 512), BF16),
+            vmem((2, 4, 2, HALF, 256), BF16),
             dma((2,)), dma, dma((2,)),
-            dma((9,)), dma((8,)), dma((8,)), dma((8,)), dma((9,)), dma((8,)), dma, dma,
+            dma((9,)), dma((STEPS, 8)), dma((8,)), dma((8,)), dma((9,)), dma((8,)), dma, dma,
             dma((STEPS,)), dma((8, STEPS)), dma((8, STEPS)),
             dma((8, STEPS)), dma((8, STEPS)), dma((8, STEPS)),
             dma((STEPS,)), dma((STEPS,)), dma((STEPS,)),
             dma((2, 2, 2)), dma((2, 2, 2)), dma((2, 4, 2)), dma((2, 4, 2)),
-            dma((2, 2)), dma((2, 2)), dma((2, 2, 2)), dma((2, 2, 2)), dma, dma,
+            dma((2, 4, 2)), dma((2, 4, 2)),
         ],
         compiler_params=pltpu.CompilerParams(
             collective_id=0, has_side_effects=True, vmem_limit_bytes=63 * 2**20

time: 135 us -> 128 us (0.948)
  Pallas kernels: 135 us -> 127 us
    pallas_call x1, Pallas kernels: 132 us -> 125 us  [local(): pl.pallas_call(kernel, out_shape=(maps, maps, jax.ShapeDtypeStruct((HALF,...]
where the time goes in v5:
time: 128 us
  Pallas kernels  127 us (99%)
    pallas_call x1, Pallas kernels, local(): pl.pallas_call(kernel, out_shape=(maps, maps, jax.ShapeDtypeStruct((HALF,...  125 us

profile of v5, /device:TPU:1, one launch (start us, length us, event | category | flops | bytes accessed | tf_op | source)
XLA Modules:
  0.0 128.1 jit_solution(11159026298194230974)
XLA Ops:
  0.6 125.3 %shard_map.58 = (bf16[6,128,256]{2,1,0:T(8,128)(2,1)}, bf16[6,128,256]{2,1,0:T(8,128)(2,1)}, f32[144,1024]{1,0:T(8,128)}) custom-call(bf16[6,128,256]{2,1,0:T(8,128)(2,1)} %bitcast.11, bf16[9,2,256,1024]{3,2,1,0:T(8,128)(2,1)} %bitcast.10, bf16[6,128,256]{2,1,0:T(8,128)(2,1)} %bitcast.12), custom_call_target="tpu_custom_call" | custom-call | tf_op jit(solution)/shard_map/pallas_call | solution.py:642
  125.9 2.2 %shard_map.59 = (bf16[6,128,256]{2,1,0:T(8,128)(2,1)}, bf16[6,128,256]{2,1,0:T(8,128)(2,1)}, f32[144,1024]{1,0:T(8,128)}) custom-call(bf16[6,128,256]{2,1,0:T(8,128)(2,1)} %get-tuple-element.9.a, bf16[6,128,256]{2,1,0:T(8,128)(2,1)} %get-tuple-element.10.b, f32[144,1024]{1,0:T(8,128)} %get-tuple-element.11.c), custom_call_target="tpu_custom_call" | custom-call | tf_op jit(solution)/shard_map/pallas_call | solution.py:705

commit v6 on v5

--- a/solution.py
+++ b/solution.py
@@ -31,10 +31,10 @@
     w, wt, acc, xc, x_rows, x_corners, xrim0, xrim1, xrim2, hs, h_rows, h_corners, hrim0, hrim1, hrim2, st, pst, act, cell, squash, up, gates, pg, hrow, gin,
     rrim0, rrim1, rrim2, urim0, urim1, urim2, grim0, grim1, grim2,
     rstage0, rstage1, rstage2, gstage0, gstage1, gstage2, gown, gsum, spread,
-    recurrent, carried, sums, part, from_l, from_r, full_l, full_r, total, got,
+    recurrent, carried, sums, part, from_l, from_r, full_l, full_r, total, from2, got,
     w_sem, in_sem, out_sem, xs_send, fr_send, hs_send, rs_send, us_send, gs_send, ps_send, pg_send,
     xc_recv, x_recv, h_recv, r_recv_rim, u_recv_rim, g_recv_rim, u_recv, ps_recv, pg_recv,
-    t_send, t_recv, f_send, f_recv, d_send, d_recv,
+    t_send, t_recv, f_send, f_recv, h2_send, h2_recv, d_send, d_recv,
 ):
     xrim, hrim, rrim = (xrim0, xrim1, xrim2), (hrim0, hrim1, hrim2), (rrim0, rrim1, rrim2)
     urim, grim = (urim0, urim1, urim2), (grim0, grim1, grim2)
@@ -103,7 +103,6 @@
             for other in range(2):
                 expected += greet(jnp.bool_(True), layer, at_ring(along_y, step, other))
 
-    acc[...] = jnp.zeros_like(acc)
     recurrent[...] = jnp.zeros_like(recurrent)
     carried[...] = jnp.zeros_like(carried)
     cell[0] = jnp.zeros((PIX, C), F32)
@@ -224,6 +223,8 @@
         rim_copies(map_rims(store, rows, corners, 0), rims, 0, send, recv, to_layer, settle)
 
     def turn_weight():
+        acc[...] = jnp.zeros_like(acc)
+
         def one(k, _):
             for n in range(2):
                 wt[n, k] = w[n, k].T
@@ -259,7 +260,7 @@
         turn_weight()
 
     def mate_patches(t):
-        return remote(st.at[t], pst.at[t], ps_send, ps_recv.at[t], layer, mate)
+        return remote(st.at[t], pst.at[t], ps_send.at[t], ps_recv.at[t], layer, mate)
 
     def above_map(t):
         return remote(hs.at[t], xc.at[t], xs_send.at[8], xc_recv.at[t], layer + 1, tile)
@@ -282,7 +283,6 @@
         def _():
             rim_arrivals(hrim, t - 1, hs_send, h_recv)
             put_rim(st.at[t, 1], hrim, t - 1)
-            mate_patches(t - 1).wait_send()
             sums[...] += jnp.dot(patches(t, 1), w[1].reshape(9 * C, GC), preferred_element_type=F32)
 
         in_gate = sigmoid(sums[:, 0:C])
@@ -308,7 +308,10 @@
             above_map(t).start()
             send_map(hs, h_rows, h_corners, xrim, t, xs_send, x_recv, layer + 1)
 
-        mate_patches(t).start()
+        @pl.when(layer == 3)
+        def _():
+            mate_patches(t).start()
+
         act[t, :, 0:C] = in_gate
         act[t, :, C : 2 * C] = forget
         act[t, :, 2 * C : 3 * C] = out_gate
@@ -324,7 +327,6 @@
         return 0
 
     lax.fori_loop(0, STEPS, forward, 0)
-    mate_patches(STEPS - 1).wait_send()
     end_map(hs, h_rows, h_corners, hrim, hs_send, h_recv, layer)
 
     hid_copy = pltpu.make_async_copy(hrow, hid_out, out_sem.at[0])
@@ -332,6 +334,11 @@
 
     @pl.when(layer < 3)
     def _():
+        def one(i, _):
+            mate_patches(STEPS - 1 - i).start()
+            return 0
+
+        lax.fori_loop(0, STEPS, one, 0)
         turn_weight()
         above_map(STEPS - 1).wait_send()
         end_map(hs, h_rows, h_corners, xrim, xs_send, x_recv, layer + 1)
@@ -508,11 +515,13 @@
             for q in range(3):
                 for n in range(2):
                     start = 512 * (3 * p + q) + C * n
-                    lhs = jnp.concatenate(
-                        [st[0, n, p, q : q + 8].reshape(PIX, C), pst[0, n, p, q : q + 8].reshape(PIX, C)], axis=0
-                    )
-                    term = lax.dot_general(lhs, rhs, (((0,), (0,)), ((), ())), preferred_element_type=F32)
-                    value = (acc[start : start + C, columns] + term).astype(BF16)
+                    value = acc[start : start + C, columns]
+                    if n == 0:
+                        lhs = jnp.concatenate(
+                            [st[0, n, p, q : q + 8].reshape(PIX, C), pst[0, n, p, q : q + 8].reshape(PIX, C)], axis=0
+                        )
+                        value += lax.dot_general(lhs, rhs, (((0,), (0,)), ((), ())), preferred_element_type=F32)
+                    value = value.astype(BF16)
                     low = start
                     while low < start + C:
                         block = low // ROWS_OUT
@@ -584,30 +593,48 @@
             layer, at_ring(n == 1, j, which),
         )
 
-    for j in (2, 1, 3, 0):
+    hand2 = {}
+    for j in (2, 3, 1, 0):
         for n in range(2):
             gather(n, j)
             if j == 0:
                 go(to_owner(n, 0, 1 - core, 0))
                 got[n, 0, core] = total[n, 0, half_rows(core), :]
+            elif j == 2:
+                for which in range(2):
+                    hand2[n, which] = go(remote(
+                        total.at[n, 2, half_rows(which)], from2.at[n, which], h2_send.at[n, which],
+                        h2_recv.at[n, which], layer, at_ring(n == 1, 1 if which == 0 else 3, core),
+                    ))
             else:
-                for which in range(2):
-                    go(to_owner(n, j, which, which))
+                which = 1 if j == 1 else 0
+                go(to_owner(n, j, which, which))
     for n in range(2):
-        remote(got.at[n, 0, 1 - core], got.at[n, 0, 1 - core], d_send.at[n, 0, 0], d_recv.at[n, 0, 1 - core], layer, mate).wait_recv()
-        for j in (1, 3, 2):
+        for which, j in ((0, 1), (1, 3)):
+            hand2[n, which].wait_recv()
+            total[n, j, half_rows(which), :] = plus(total[n, j, half_rows(which), :], from2[n, which])
+            go(to_owner(n, j, which, which))
+    for n in range(2):
+        here = got.at[n, 0, 1 - core]
+        remote(here, here, d_send.at[n, 0, 0], d_recv.at[n, 0, 1 - core], layer, mate).wait_recv()
+        for j in (1, 3):
             for which in range(2):
                 here = got.at[n, j, which]
                 remote(here, here, d_send.at[n, j, which], d_recv.at[n, j, which], layer, at_ring(n == 1, 4 - j, which)).wait_recv()
     for which in range(2):
         for n in range(2):
             low = 512 * which + 256 * n
-            wg_out[:, low : low + 256] = (got[n, 0, which].astype(F32) + got[n, 1, which].astype(F32)) + (
-                got[n, 2, which].astype(F32) + got[n, 3, which].astype(F32)
+            wg_out[:, low : low + 256] = (
+                got[n, 0, which].astype(F32) + got[n, 1, which].astype(F32) + got[n, 3, which].astype(F32)
             )
     for copy in sent:
         copy.wait_send()
 
+    def left(t, _):
+        mate_patches(t).wait_send()
+        return 0
+
+    lax.fori_loop(0, STEPS, left, 0)
     hid_copy.wait()
     gin_copy.wait()
 
@@ -685,14 +712,15 @@
             vmem((2, 4) + block, BF16),
             vmem((2, 4) + block, BF16),
             vmem((2, 4) + block, BF16),
+            vmem((2, 2, HALF, 256), BF16),
             vmem((2, 4, 2, HALF, 256), BF16),
             dma((2,)), dma, dma((2,)),
-            dma((9,)), dma((STEPS, 8)), dma((8,)), dma((8,)), dma((9,)), dma((8,)), dma, dma,
+            dma((9,)), dma((STEPS, 8)), dma((8,)), dma((8,)), dma((9,)), dma((8,)), dma((STEPS,)), dma,
             dma((STEPS,)), dma((8, STEPS)), dma((8, STEPS)),
             dma((8, STEPS)), dma((8, STEPS)), dma((8, STEPS)),
             dma((STEPS,)), dma((STEPS,)), dma((STEPS,)),
             dma((2, 2, 2)), dma((2, 2, 2)), dma((2, 4, 2)), dma((2, 4, 2)),
-            dma((2, 4, 2)), dma((2, 4, 2)),
+            dma((2, 2)), dma((2, 2)), dma((2, 4, 2)), dma((2, 4, 2)),
         ],
         compiler_params=pltpu.CompilerParams(
             collective_id=0, has_side_effects=True, vmem_limit_bytes=63 * 2**20

time: 128 us -> 126 us (0.984)
  Pallas kernels: 127 us -> 125 us
    pallas_call x1, Pallas kernels: 125 us -> 123 us  [local(): pl.pallas_call(kernel, out_shape=(maps, maps, jax.ShapeDtypeStruct((HALF,...]
where the time goes in v6:
time: 126 us
  Pallas kernels  125 us (99%)
    pallas_call x1, Pallas kernels, local(): pl.pallas_call(kernel, out_shape=(maps, maps, jax.ShapeDtypeStruct((HALF,...  123 us

profile of v6, /device:TPU:1, one launch (start us, length us, event | category | flops | bytes accessed | tf_op | source)
XLA Modules:
  0.0 125.9 jit_solution(17869628240922733184)
XLA Ops:
  0.6 123.1 %shard_map.58 = (bf16[6,128,256]{2,1,0:T(8,128)(2,1)}, bf16[6,128,256]{2,1,0:T(8,128)(2,1)}, f32[144,1024]{1,0:T(8,128)}) custom-call(bf16[6,128,256]{2,1,0:T(8,128)(2,1)} %bitcast.11, bf16[9,2,256,1024]{3,2,1,0:T(8,128)(2,1)} %bitcast.10, bf16[6,128,256]{2,1,0:T(8,128)(2,1)} %bitcast.12), custom_call_target="tpu_custom_call" | custom-call | tf_op jit(solution)/shard_map/pallas_call | solution.py:669
  123.7 2.2 %shard_map.59 = (bf16[6,128,256]{2,1,0:T(8,128)(2,1)}, bf16[6,128,256]{2,1,0:T(8,128)(2,1)}, f32[144,1024]{1,0:T(8,128)}) custom-call(bf16[6,128,256]{2,1,0:T(8,128)(2,1)} %get-tuple-element.9.a, bf16[6,128,256]{2,1,0:T(8,128)(2,1)} %get-tuple-element.10.b, f32[144,1024]{1,0:T(8,128)} %get-tuple-element.11.c), custom_call_target="tpu_custom_call" | custom-call | tf_op jit(solution)/shard_map/pallas_call | solution.py:733

commit v7 on v6

--- a/solution.py
+++ b/solution.py
@@ -18,6 +18,7 @@
 ROWS_OUT = 288
 HALF = 144
 FORGET_SHIFT = 1.0
+CUTS = tuple(slice(low, low + 32) for low in range(0, PIX, 32))
 PIECE = ((2, 0), (1, 0), (2, 1), (0, 0), (0, 1), (2, 2), (1, 1), (2, 3))
 DIRS = ((-1, -1), (-1, 0), (-1, 1), (0, -1), (0, 1), (1, -1), (1, 0), (1, 1))
 
@@ -285,13 +286,22 @@
             put_rim(st.at[t, 1], hrim, t - 1)
             sums[...] += jnp.dot(patches(t, 1), w[1].reshape(9 * C, GC), preferred_element_type=F32)
 
-        in_gate = sigmoid(sums[:, 0:C])
-        forget = sigmoid(sums[:, C : 2 * C] + FORGET_SHIFT)
-        out_gate = sigmoid(sums[:, 2 * C : 3 * C])
-        update = jnp.tanh(sums[:, 3 * C :])
-        fresh = forget * cell[t] + in_gate * update
-        squashed = jnp.tanh(fresh)
-        hidden = out_gate * squashed
+        pieces = []
+        for cut in CUTS:
+            in_gate = sigmoid(sums[cut, 0:C])
+            forget = sigmoid(sums[cut, C : 2 * C] + FORGET_SHIFT)
+            out_gate = sigmoid(sums[cut, 2 * C : 3 * C])
+            update = jnp.tanh(sums[cut, 3 * C :])
+            fresh = forget * cell[t, cut] + in_gate * update
+            squashed = jnp.tanh(fresh)
+            pieces.append(out_gate * squashed)
+            act[t, cut, 0:C] = in_gate
+            act[t, cut, C : 2 * C] = forget
+            act[t, cut, 2 * C : 3 * C] = out_gate
+            act[t, cut, 3 * C :] = update
+            cell[t + 1, cut] = fresh
+            squash[t, cut] = squashed
+        hidden = jnp.concatenate(pieces, axis=0)
         hs[t] = hidden.astype(BF16).reshape(COLS, ROWS, C)
         put_stage(h_rows, h_corners, t, hidden)
 
@@ -312,12 +322,6 @@
         def _():
             mate_patches(t).start()
 
-        act[t, :, 0:C] = in_gate
-        act[t, :, C : 2 * C] = forget
-        act[t, :, 2 * C : 3 * C] = out_gate
-        act[t, :, 3 * C :] = update
-        cell[t + 1] = fresh
-        squash[t] = squashed
         hrow[t] = by_rows(hidden)
 
         @pl.when(t < STEPS - 1)
@@ -441,17 +445,19 @@
             rim_arrivals(urim, t, us_send, u_recv_rim)
 
         grad_hidden = add_rims(up[t].astype(F32).reshape(PIX, C) + recurrent[...], urim, t)
-        in_gate = act[t, :, 0:C]
-        forget = act[t, :, C : 2 * C]
-        out_gate = act[t, :, 2 * C : 3 * C]
-        update = act[t, :, 3 * C :]
-        squashed = squash[t]
-        grad_cell = grad_hidden * out_gate * (1.0 - squashed * squashed) + carried[...]
-        carried[...] = grad_cell * forget
-        gates[t, :, 0:C] = (grad_cell * update * in_gate * (1.0 - in_gate)).astype(BF16)
-        gates[t, :, C : 2 * C] = (grad_cell * cell[t] * forget * (1.0 - forget)).astype(BF16)
-        gates[t, :, 2 * C : 3 * C] = (grad_hidden * squashed * out_gate * (1.0 - out_gate)).astype(BF16)
-        gates[t, :, 3 * C :] = (grad_cell * in_gate * (1.0 - update * update)).astype(BF16)
+        for cut in CUTS:
+            arrived = grad_hidden[cut]
+            in_gate = act[t, cut, 0:C]
+            forget = act[t, cut, C : 2 * C]
+            out_gate = act[t, cut, 2 * C : 3 * C]
+            update = act[t, cut, 3 * C :]
+            squashed = squash[t, cut]
+            grad_cell = arrived * out_gate * (1.0 - squashed * squashed) + carried[cut]
+            carried[cut] = grad_cell * forget
+            gates[t, cut, 0:C] = (grad_cell * update * in_gate * (1.0 - in_gate)).astype(BF16)
+            gates[t, cut, C : 2 * C] = (grad_cell * cell[t, cut] * forget * (1.0 - forget)).astype(BF16)
+            gates[t, cut, 2 * C : 3 * C] = (arrived * squashed * out_gate * (1.0 - out_gate)).astype(BF16)
+            gates[t, cut, 3 * C :] = (grad_cell * in_gate * (1.0 - update * update)).astype(BF16)
 
         @pl.when(i > 0)
         def _():
@@ -506,31 +512,30 @@
     hand = {}
     full = {}
 
-    def last_terms(half):
+    def last_terms(half, n):
         columns = slice(256 * half, 256 * half + 256)
-        rhs = jnp.concatenate(
-            [gates[0, :, pl.ds(pl.multiple_of(core * 512 + 256 * half, 256), 256)], pg[0, :, columns]], axis=0
-        )
+        if n == 0:
+            mine_now = pl.ds(pl.multiple_of(core * 512 + 256 * half, 256), 256)
+            rhs = jnp.concatenate([gates[0, :, mine_now], pg[0, :, columns]], axis=0)
         for p in range(3):
             for q in range(3):
-                for n in range(2):
-                    start = 512 * (3 * p + q) + C * n
-                    value = acc[start : start + C, columns]
-                    if n == 0:
-                        lhs = jnp.concatenate(
-                            [st[0, n, p, q : q + 8].reshape(PIX, C), pst[0, n, p, q : q + 8].reshape(PIX, C)], axis=0
-                        )
-                        value += lax.dot_general(lhs, rhs, (((0,), (0,)), ((), ())), preferred_element_type=F32)
-                    value = value.astype(BF16)
-                    low = start
-                    while low < start + C:
-                        block = low // ROWS_OUT
-                        high = min(start + C, ROWS_OUT * (block + 1))
-                        rows = slice(low - ROWS_OUT * block, high - ROWS_OUT * block)
-                        z, y = block // 4, block % 4
-                        at = (0, y, z, rows) if half == 0 else (1, z, y, rows)
-                        part[at] = value[low - start : high - start]
-                        low = high
+                start = 512 * (3 * p + q) + C * n
+                value = acc[start : start + C, columns]
+                if n == 0:
+                    lhs = jnp.concatenate(
+                        [st[0, n, p, q : q + 8].reshape(PIX, C), pst[0, n, p, q : q + 8].reshape(PIX, C)], axis=0
+                    )
+                    value += lax.dot_general(lhs, rhs, (((0,), (0,)), ((), ())), preferred_element_type=F32)
+                value = value.astype(BF16)
+                low = start
+                while low < start + C:
+                    block = low // ROWS_OUT
+                    high = min(start + C, ROWS_OUT * (block + 1))
+                    rows = slice(low - ROWS_OUT * block, high - ROWS_OUT * block)
+                    z, y = block // 4, block % 4
+                    at = (0, y, z, rows) if half == 0 else (1, z, y, rows)
+                    part[at] = value[low - start : high - start]
+                    low = high
 
     def send_full(n, j, right):
         a, b = own(n)
@@ -539,11 +544,13 @@
             f_send.at[n, j, int(right)], f_recv.at[n, j, int(right)], layer, at_ring(n == 0, 1 if right else 3, core),
         ))
 
+    for half in range(2):
+        last_terms(half, 1)
     wait_mate(0)
     mate_gates(0).wait_send()
     for n in range(2):
         a, b = own(n)
-        last_terms(n)
+        last_terms(n, 0)
         for m in range(2):
             for right in (True, False):
                 j = (rights if right else lefts)[m]

time: 126 us -> 126 us (level)
  no operation moved by 1% of the time
where the time goes in v7:
time: 126 us; the launch traced here: 125 us
  Pallas kernels  125 us (99%)
    pallas_call x1, Pallas kernels, local(): pl.pallas_call(kernel, out_shape=(maps, maps, jax.ShapeDtypeStruct((HALF,...  123 us

profile of v7, /device:TPU:1, one launch (start us, length us, event | category | flops | bytes accessed | tf_op | source)
XLA Modules:
  0.0 125.5 jit_solution(5029668468067205308)
XLA Ops:
  0.6 122.7 %shard_map.58 = (bf16[6,128,256]{2,1,0:T(8,128)(2,1)}, bf16[6,128,256]{2,1,0:T(8,128)(2,1)}, f32[144,1024]{1,0:T(8,128)}) custom-call(bf16[6,128,256]{2,1,0:T(8,128)(2,1)} %bitcast.11, bf16[9,2,256,1024]{3,2,1,0:T(8,128)(2,1)} %bitcast.10, bf16[6,128,256]{2,1,0:T(8,128)(2,1)} %bitcast.12), custom_call_target="tpu_custom_call" | custom-call | tf_op jit(solution)/shard_map/pallas_call | solution.py:676
  123.3 2.2 %shard_map.59 = (bf16[6,128,256]{2,1,0:T(8,128)(2,1)}, bf16[6,128,256]{2,1,0:T(8,128)(2,1)}, f32[144,1024]{1,0:T(8,128)}) custom-call(bf16[6,128,256]{2,1,0:T(8,128)(2,1)} %get-tuple-element.9.a, bf16[6,128,256]{2,1,0:T(8,128)(2,1)} %get-tuple-element.10.b, f32[144,1024]{1,0:T(8,128)} %get-tuple-element.11.c), custom_call_target="tpu_custom_call" | custom-call | tf_op jit(solution)/shard_map/pallas_call | solution.py:740

commit v8 on v7

--- a/solution.py
+++ b/solution.py
@@ -263,17 +263,31 @@
     def mate_patches(t):
         return remote(st.at[t], pst.at[t], ps_send.at[t], ps_recv.at[t], layer, mate)
 
-    def above_map(t):
-        return remote(hs.at[t], xc.at[t], xs_send.at[8], xc_recv.at[t], layer + 1, tile)
+    def above_map(t, half):
+        columns = pl.ds(4 * half, 4)
+        return remote(
+            hs.at[t, columns], xc.at[t, columns], xs_send.at[8 + half], xc_recv.at[t, half], layer + 1, tile
+        )
 
     def patches(t, n):
         taps = [st[t, n, p, q : q + 8].reshape(PIX, C) for p in range(3) for q in range(3)]
         return jnp.concatenate(taps, axis=1)
 
+    def send_above(t, half):
+        @pl.when(layer < 3)
+        def _():
+            @pl.when(t > 0)
+            def _():
+                above_map(t - 1, half).wait_send()
+
+            above_map(t, half).start()
+
     def forward(t, _):
         @pl.when(layer > 0)
         def _():
-            remote(xc.at[t], xc.at[t], xs_send.at[8], xc_recv.at[t], layer - 1, tile).wait_recv()
+            for half in range(2):
+                here = xc.at[t, pl.ds(4 * half, 4)]
+                remote(here, here, xs_send.at[8 + half], xc_recv.at[t, half], layer - 1, tile).wait_recv()
 
         put_centre(st.at[t, 0], xc[t].astype(F32).reshape(PIX, C))
         rim_arrivals(xrim, t, xs_send, x_recv)
@@ -287,7 +301,7 @@
             sums[...] += jnp.dot(patches(t, 1), w[1].reshape(9 * C, GC), preferred_element_type=F32)
 
         pieces = []
-        for cut in CUTS:
+        for m, cut in enumerate(CUTS):
             in_gate = sigmoid(sums[cut, 0:C])
             forget = sigmoid(sums[cut, C : 2 * C] + FORGET_SHIFT)
             out_gate = sigmoid(sums[cut, 2 * C : 3 * C])
@@ -301,21 +315,20 @@
             act[t, cut, 3 * C :] = update
             cell[t + 1, cut] = fresh
             squash[t, cut] = squashed
+            hs[t, 2 * m : 2 * m + 2] = pieces[m].astype(BF16).reshape(2, ROWS, C)
+            if m == 1:
+                send_above(t, 0)
         hidden = jnp.concatenate(pieces, axis=0)
-        hs[t] = hidden.astype(BF16).reshape(COLS, ROWS, C)
         put_stage(h_rows, h_corners, t, hidden)
 
         @pl.when(t < STEPS - 1)
         def _():
             send_map(hs, h_rows, h_corners, hrim, t, hs_send, h_recv, layer)
 
+        send_above(t, 1)
+
         @pl.when(layer < 3)
         def _():
-            @pl.when(t > 0)
-            def _():
-                above_map(t - 1).wait_send()
-
-            above_map(t).start()
             send_map(hs, h_rows, h_corners, xrim, t, xs_send, x_recv, layer + 1)
 
         @pl.when(layer == 3)
@@ -344,7 +357,8 @@
 
         lax.fori_loop(0, STEPS, one, 0)
         turn_weight()
-        above_map(STEPS - 1).wait_send()
+        for half in range(2):
+            above_map(STEPS - 1, half).wait_send()
         end_map(hs, h_rows, h_corners, xrim, xs_send, x_recv, layer + 1)
 
     @pl.when(layer == 0)
@@ -722,8 +736,8 @@
             vmem((2, 2, HALF, 256), BF16),
             vmem((2, 4, 2, HALF, 256), BF16),
             dma((2,)), dma, dma((2,)),
-            dma((9,)), dma((STEPS, 8)), dma((8,)), dma((8,)), dma((9,)), dma((8,)), dma((STEPS,)), dma,
-            dma((STEPS,)), dma((8, STEPS)), dma((8, STEPS)),
+            dma((10,)), dma((STEPS, 8)), dma((8,)), dma((8,)), dma((9,)), dma((8,)), dma((STEPS,)), dma,
+            dma((STEPS, 2)), dma((8, STEPS)), dma((8, STEPS)),
             dma((8, STEPS)), dma((8, STEPS)), dma((8, STEPS)),
             dma((STEPS,)), dma((STEPS,)), dma((STEPS,)),
             dma((2, 2, 2)), dma((2, 2, 2)), dma((2, 4, 2)), dma((2, 4, 2)),

time: 126 us -> 125 us (level)
  no operation moved by 1% of the time
where the time goes in v8:
time: 125 us
  Pallas kernels  125 us (100%)
    pallas_call x1, Pallas kernels, local(): pl.pallas_call(kernel, out_shape=(maps, maps, jax.ShapeDtypeStruct((HALF,...  122 us

profile of v8, /device:TPU:1, one launch (start us, length us, event | category | flops | bytes accessed | tf_op | source)
XLA Modules:
  0.0 125.2 jit_solution(13297427603508970966)
XLA Ops:
  0.6 122.4 %shard_map.58 = (bf16[6,128,256]{2,1,0:T(8,128)(2,1)}, bf16[6,128,256]{2,1,0:T(8,128)(2,1)}, f32[144,1024]{1,0:T(8,128)}) custom-call(bf16[6,128,256]{2,1,0:T(8,128)(2,1)} %bitcast.11, bf16[9,2,256,1024]{3,2,1,0:T(8,128)(2,1)} %bitcast.10, bf16[6,128,256]{2,1,0:T(8,128)(2,1)} %bitcast.12), custom_call_target="tpu_custom_call" | custom-call | tf_op jit(solution)/shard_map/pallas_call | solution.py:690
  123.1 2.2 %shard_map.59 = (bf16[6,128,256]{2,1,0:T(8,128)(2,1)}, bf16[6,128,256]{2,1,0:T(8,128)(2,1)}, f32[144,1024]{1,0:T(8,128)}) custom-call(bf16[6,128,256]{2,1,0:T(8,128)(2,1)} %get-tuple-element.9.a, bf16[6,128,256]{2,1,0:T(8,128)(2,1)} %get-tuple-element.10.b, f32[144,1024]{1,0:T(8,128)} %get-tuple-element.11.c), custom_call_target="tpu_custom_call" | custom-call | tf_op jit(solution)/shard_map/pallas_call | solution.py:754
